TPU v7x, 512 devices: a whole 4x8x8 slice. The times are simulated.
512 devices in a mesh: vocab: 128 (over z, y, core), rows: 4 (over x).
Axes of the slice: x: 4, y: 8, z: 8, core: 2. Of those that a mesh axis runs over, the one named last changes fastest.
Arguments:
- target_hidden: bfloat16 [256, 8192], P('vocab', 'rows'), may hold values from -70 to 70
- target_head: bfloat16 [81920, 8192], P('vocab', 'rows'), may hold values from -0.1875 to 0.1875
- draft_hidden: bfloat16 [256, 8192], P('vocab', 'rows'), may hold values from -70 to 70
- draft_head: bfloat16 [32768, 8192], P('vocab', 'rows'), may hold values from -0.1875 to 0.1875
- draft_map: int32 [32768], P('vocab'), may hold values from 0 to 40959, as said below
- draft_valid: int32 [32768], P('vocab'), may hold values 0 or 1
- loss_scale: float32 [], replicated, may hold values from 2048 to 8192
Outputs:
- row_loss: float32 [256], P('rows')
- grad_hidden: bfloat16 [256, 8192], P('vocab', 'rows')
- grad_head: bfloat16 [32768, 8192], P('vocab', 'rows')
Inputs may be any that keep to these rules, and one draw needn't show every extreme that they name: `draft_map`: each aligned block of 128 draft ids maps one to one onto the 128 ids of one target tile (target ids 128 t to 128 t + 127); the target tile rises strictly from block to block; every index of vocab below half of the axis owns exactly 4 used target tiles, the other indices none; the last of the owning indices always uses its highest tile.
All inputs are finite; a program needn't handle non-finite values. No bound on the sum of `draft_valid` on one device may be relied on, other than what follows from the above.
Results may differ from a plain program's by a relative error of at most 0.0225.
Values may be sent and summed in bfloat16 or wider, within the bound.
A program may use at most 64 MiB of HBM per device.

v0:
```python
import jax
import jax.numpy as jnp
from jax import lax
from jax.sharding import PartitionSpec as P

TILE = 128
SEND_CAP = 4


far_below = -1e30


def on_device(
    target_hidden, target_head, draft_hidden, draft_head, draft_map, draft_valid, loss_scale
):
    n_vocab = lax.axis_size("vocab")
    vocab_index = lax.axis_index("vocab")
    tile_width = TILE
    vt_local = target_head.shape[0]
    vd_local = draft_head.shape[0]
    tiles_target = vt_local // tile_width
    tiles_draft = vd_local // tile_width
    contract = (((1,), (1,)), ((), ()))
    target_all, draft_all = (
        lax.all_gather(target_hidden, "vocab", axis=0, tiled=True),
        lax.all_gather(draft_hidden, "vocab", axis=0, tiled=True),
    )
    sources = draft_map.reshape(tiles_draft, tile_width)[:, 0] // tile_width
    source_table = lax.all_gather(sources, "vocab", axis=0, tiled=True)
    target_part = lax.dot_general(
        target_all, target_head, contract, preferred_element_type=jnp.float32
    )
    target_logits = lax.psum_scatter(target_part, "rows", scatter_dimension=0, tiled=True)
    draft_part = lax.dot_general(
        draft_all, draft_head, contract, preferred_element_type=jnp.float32
    )
    draft_logits = lax.psum_scatter(draft_part, "rows", scatter_dimension=0, tiled=True)
    rows_here = target_logits.shape[0]
    live_limit = vt_local * n_vocab - vt_local // 2
    live_cols = (vocab_index * vt_local + jnp.arange(vt_local) < live_limit)[None, :]
    valid_cols = (draft_valid > 0)[None, :]
    target_local = jnp.max(jnp.where(live_cols, target_logits, far_below), axis=1)
    draft_local = jnp.max(jnp.where(valid_cols, draft_logits, far_below), axis=1)
    target_max, draft_max = lax.pmax((target_local, draft_local), "vocab")
    target_part_sum = jnp.sum(
        jnp.where(live_cols, jnp.exp(target_logits - target_max[:, None]), 0.0), axis=1
    )
    draft_part_sum = jnp.sum(
        jnp.where(valid_cols, jnp.exp(draft_logits - draft_max[:, None]), 0.0), axis=1
    )
    target_total, draft_total = lax.psum((target_part_sum, draft_part_sum), "vocab")
    target_exp = jnp.where(live_cols, jnp.exp(target_logits - target_max[:, None]), 0.0)
    target_prob = (target_exp / target_total[:, None]).astype(jnp.bfloat16)
    prob_tiles = target_prob.reshape(rows_here, tiles_target, tile_width)
    owner_dev = source_table // tiles_target
    local_tile = source_table - owner_dev * tiles_target
    positions = jnp.arange(source_table.shape[0])
    earlier = (owner_dev[None, :] == owner_dev[:, None]) & (positions[None, :] < positions[:, None])
    slot_rank = jnp.sum(earlier.astype(jnp.int32), axis=1)
    owned_here = owner_dev == vocab_index
    my_tiles = vocab_index * tiles_draft + jnp.arange(tiles_draft)
    slot_ids = jnp.arange(SEND_CAP)
    slot_match = owned_here[None, :] & (slot_rank[None, :] == slot_ids[:, None])
    chosen = jnp.sum(jnp.where(slot_match, local_tile[None, :], 0), axis=1)
    filled = jnp.any(slot_match, axis=1)
    picked = jnp.take(prob_tiles, chosen, axis=1)
    outgoing = jnp.where(filled[None, :, None], picked, jnp.zeros_like(picked))
    incoming = lax.all_gather(outgoing, "vocab", axis=1, tiled=True)
    slot_index = owner_dev[my_tiles] * SEND_CAP + slot_rank[my_tiles]
    arrived = jnp.take(incoming, slot_index, axis=1)
    column_pick = draft_map.reshape(tiles_draft, tile_width) % tile_width
    selector = (column_pick[:, :, None] == jnp.arange(tile_width)[None, None, :]).astype(
        jnp.bfloat16
    )
    soft_block = jnp.einsum("rjk,jck->rjc", arrived, selector, preferred_element_type=jnp.float32)
    soft_target = jnp.where(valid_cols, soft_block.reshape(rows_here, vd_local), 0.0).astype(
        jnp.bfloat16
    )
    soft_wide = soft_target.astype(jnp.float32)
    target_mass, cross_term = lax.psum(
        (jnp.sum(soft_wide, axis=1), jnp.sum(soft_wide * draft_logits, axis=1)), "vocab"
    )
    draft_lse = draft_max + jnp.log(draft_total)
    row_loss = target_mass * draft_lse - cross_term
    grad_value = loss_scale * (
        jnp.exp(draft_logits - draft_lse[:, None]) * target_mass[:, None] - soft_wide
    )
    logit_grad = jnp.where(valid_cols, grad_value, 0.0).astype(jnp.bfloat16)
    grad_all = lax.all_gather(logit_grad, "rows", axis=0, tiled=True)
    grad_head = lax.dot_general(
        grad_all, draft_all, (((0,), (0,)), ((), ())), preferred_element_type=jnp.float32
    ).astype(jnp.bfloat16)
    grad_hidden = lax.psum_scatter(
        jnp.dot(grad_all, draft_head, preferred_element_type=jnp.float32),
        "vocab",
        scatter_dimension=0,
        tiled=True,
    ).astype(jnp.bfloat16)
    return (row_loss, grad_hidden, grad_head)


def solution(mesh):
    in_specs = (
        P("vocab", "rows"),
        P("vocab", "rows"),
        P("vocab", "rows"),
        P("vocab", "rows"),
        P("vocab"),
        P("vocab"),
        P(),
    )
    out_specs = (P("rows"), P("vocab", "rows"), P("vocab", "rows"))
    return jax.shard_map(
        on_device, mesh=mesh, in_specs=in_specs, out_specs=out_specs, check_vma=False
    )
```

profile of v0, /device:TPU:1, one launch (start us, length us, event | category | flops | bytes accessed | tf_op | source)
XLA Modules:
  0.0 1601.3 jit_solution(17588961918025539512)
XLA Ops:
  7.2 0.0 copy-start
  7.2 0.0 all-gather.10.cloned.1.call-start
  7.2 0.7 all-gather.10.cloned.1.call-update
  7.9 0.0 all-gather.8.cloned.1.call-start
  8.0 0.7 all-gather.8.cloned.1.call-update
  8.7 0.0 reduce-scatter.5.cloned.1.call-start
  8.7 1.4 fusion.23
  10.7 0.8 slice_reduce_fusion
  11.5 0.1 fusion.21
  11.6 27.8 %all-reduce = s32[256]{0:T(256)S(1)} all-reduce(s32[256]{0:T(256)S(1)} %fusion.21), channel_id=1, replica_groups=mesh['vocab'=128,'rows'=4] {'vocab'}, use_global_device_ids=true, to_apply=%add | all-reduce | flops 256 | bytes 2048
  39.4 56.8 %all-gather.10.cloned.1.call-done = bf16[128,2,2048]{2,1,0:T(2,128)(2,1)} async-done(((bf16[1,2,2048]{2,1,0:T(2,128)(2,1)}), bf16[128,2,2048]{2,1,0:T(2,128)(2,1)}) %all-gather.10.cloned.1.call-update) | async-done | bytes 1048592 | tf_op jit(solution)/shard_map/all_gather | solution.py:26
  96.2 2.2 reshape.166
  98.5 2.7 fusion.25
  101.2 0.0 reduce-scatter.5.cloned.1.call-update
  101.2 0.0 reduce-scatter.3.cloned.1.call-start
  101.3 0.2 convert_reduce_fusion
  101.5 72.7 %all-gather.8.cloned.1.call-done = bf16[128,2,2048]{2,1,0:T(2,128)(2,1)} async-done(((bf16[1,2,2048]{2,1,0:T(2,128)(2,1)}), bf16[128,2,2048]{2,1,0:T(2,128)(2,1)}) %all-gather.8.cloned.1.call-update) | async-done | bytes 1048592 | tf_op jit(solution)/shard_map/all_gather | solution.py:25
  174.2 2.3 reshape.164
  176.5 0.0 copy-done
  176.5 0.0 copy-start.3
  176.5 0.0 copy-start.2
  176.5 3.1 fusion.24
  179.6 0.0 reduce-scatter.3.cloned.1.call-update
  179.6 0.0 all-gather.6.cloned.1.call-start
  179.7 0.1 select_reduce_fusion.3
  179.8 0.1 fusion.16
  179.9 0.0 copy-done.3
  180.0 16.0 reduce-scatter.5.cloned.1.call-done
  196.0 0.9 select_reduce_fusion.2
  196.9 29.5 %reduce-scatter.3.cloned.1.call-done = f32[64,640]{1,0:T(8,128)} async-done(((f32[256,640]{1,0:T(8,128)}), f32[64,640]{1,0:T(8,128)}) %reduce-scatter.3.cloned.1.call-update) | async-done | bytes 163856 | tf_op jit(solution)/shard_map/reduce_scatter | solution.py:33
  226.4 1.0 select_reduce_fusion
  227.5 249.8 %all-reduce.4 = (f32[64]{0:T(128)S(1)}, f32[64]{0:T(128)S(1)}) all-reduce(f32[64]{0:T(128)S(1)} %select_reduce_fusion.2, f32[64]{0:T(128)S(1)} %select_reduce_fusion), channel_id=1, replica_groups=mesh['vocab'=128,'rows'=4] {'vocab'}, use_global_device_ids=true, to_apply=%region_12.13 | all-reduce | flops 128 | bytes 1024 | tf_op jit(solution)/shard_map/pmax | solution.py:44
  477.2 1.1 fusion.1
  478.4 250.0 %psum.28 = f32[64]{0:T(128)S(1)} all-reduce(f32[64]{0:T(128)S(1)} %fusion.1), channel_id=1, replica_groups=mesh['vocab'=128,'rows'=4] {'vocab'}, use_global_device_ids=true, to_apply=%region_7.8 | all-reduce | flops 64 | bytes 512 | tf_op jit(solution)/shard_map/psum | solution.py:51
  728.4 1.0 copy_bitcast_fusion
  729.4 0.6 gather_fusion.2
  730.0 0.7 select_bitcast_fusion
  730.7 0.0 all-gather.6.cloned.1.call-update
  730.7 0.6 gather_fusion.1
  731.4 0.6 gather_fusion
  733.4 0.0 copy-done.2
  733.4 77.3 %all-gather.6.cloned.1.call-done = bf16[64,512,128]{2,0,1:T(8,128)(2,1)} async-done(((bf16[64,4,128]{2,0,1:T(8,128)(2,1)}), bf16[64,512,128]{2,0,1:T(8,128)(2,1)}) %all-gather.6.cloned.1.call-update) | async-done | bytes 8388624 | tf_op jit(solution)/shard_map/all_gather | solution.py:68
  810.7 3.9 gather_fusion.3
  814.7 0.3 convert_reduce_fusion.1
  815.0 1.0 select_reduce_fusion.1
  816.0 246.4 %all-reduce.3 = (f32[64]{0:T(128)S(1)}, f32[64]{0:T(128)S(1)}) all-reduce(f32[64]{0:T(128)S(1)} %get-tuple-element.15, f32[64]{0:T(128)S(1)} %get-tuple-element.3), channel_id=1, replica_groups=mesh['vocab'=128,'rows'=4] {'vocab'}, use_global_device_ids=true, to_apply=%region_9.10 | all-reduce | flops 128 | bytes 1024 | tf_op jit(solution)/shard_map/psum | solution.py:80
  1062.4 0.0 copy-start.1
  1062.5 1.0 fusion.7
  1063.5 9.4 all_gather.19
  1072.9 3.0 fusion.26
  1075.9 0.0 copy-done.1
  1075.9 1.4 convolution_convert_fusion
  1077.3 515.6 %all-reduce.6 = (f32[64]{0:T(128)S(1)}, bf16[256,2048]{1,0:T(8,128)(2,1)}) all-reduce(f32[64]{0:T(128)S(1)} %get-tuple-element.4, f32[256,2048]{1,0:T(8,128)} %fusion.26), channel_id=1, replica_groups=mesh['vocab'=128,'rows'=4] {'vocab'}, use_global_device_ids=true, to_apply=%region_16.17 | all-reduce | flops 524352 | bytes 3146240 | tf_op jit(solution)/shard_map/psum | solution.py:80
  1592.9 0.5 multiply_subtract_fusion.1
  1593.4 1.4 dynamic-slice_convert_fusion
  (16 shorter events, 0.1 us)
Async XLA Ops:
  7.2 169.3 %copy-start = (bf16[640,2048]{1,0:T(8,128)(2,1)S(1)}, bf16[640,2048]{1,0:T(8,128)(2,1)}, u32[]{:S(2)}) copy-start(bf16[640,2048]{1,0:T(8,128)(2,1)} %param.8) | copy-start | bytes 7864324
  7.2 89.1 %all-gather.10.cloned.1.call-start = ((), (), s32[]{:S(2)}) async-start(), calls=%async_computation.6 | async-start | bytes 1056768 | tf_op jit(solution)/shard_map/all_gather | solution.py:26
  7.9 166.3 %all-gather.8.cloned.1.call-start = ((), (), s32[]{:S(2)}) async-start(), calls=%async_computation.5 | async-start | bytes 1056768 | tf_op jit(solution)/shard_map/all_gather | solution.py:25
  8.7 187.3 %reduce-scatter.5.cloned.1.call-start = ((), (), s32[]{:S(2)}) async-start(), calls=%async_computation.4 | async-start | bytes 327680 | tf_op jit(solution)/shard_map/reduce_scatter | solution.py:37
  101.2 125.2 %reduce-scatter.3.cloned.1.call-start = ((), (), s32[]{:S(2)}) async-start(), calls=%async_computation.2 | async-start | bytes 819200 | tf_op jit(solution)/shard_map/reduce_scatter | solution.py:33
  176.5 3.5 copy-start.3
  176.5 556.9 %copy-start.2 = (s32[256]{0:T(256)S(1)}, s32[256]{0:T(256)}, u32[]{:S(2)}) copy-start(s32[256]{0:T(256)} %param.11) | copy-start | bytes 3076
  179.6 631.1 %all-gather.6.cloned.1.call-start = ((), (), s32[]{:S(2)}) async-start(), calls=%async_computation.3 | async-start | bytes 8454144 | tf_op jit(solution)/shard_map/all_gather | solution.py:68
  1062.4 13.5 copy-start.1
Sparse Core Ops, SparseCore 0:
  11.0 85.1 all-gather.9
  99.3 74.8 all-gather.7
  177.0 18.9 reduce-scatter.4
  198.9 27.5 reduce-scatter.2
  730.8 79.8 all-gather.5
where the time goes:
time: 1610 us; the launch traced here: 1600 us
  blocking collectives  1300 us (81%)
  waiting for transfers between devices  254 us (16%)
    psum x2, blocking collectives, on_device(): lax.psum((jnp.sum(soft_wide, axis=1), jnp.sum(soft_wide * draft_logits, a...  762 us
    psum x1, blocking collectives, on_device(): lax.psum((target_part_sum, draft_part_sum), 'vocab')  250 us
    pmax x1, blocking collectives, on_device(): target_max, draft_max = lax.pmax((target_local, draft_local), 'vocab')  250 us
    all_gather x1, waiting for transfers between devices, on_device(): incoming = lax.all_gather(outgoing, 'vocab', axis=1, tiled=True)  77.3 us
    all_gather x1, waiting for transfers between devices, on_device(): lax.all_gather(target_hidden, 'vocab', axis=0, tiled=True)  72.7 us
    all_gather x1, waiting for transfers between devices, on_device(): lax.all_gather(draft_hidden, 'vocab', axis=0, tiled=True)  56.8 us
  transfers between devices with their start and end apart: 5, of which 5 were waited for; matrix products, arithmetic and copies ran while one was open for 1% of the time, Pallas kernels for 0%

commit v1 on v0

v1 whole, which is shorter than its diff:
```python
import functools
import math

import jax
import jax.numpy as jnp
from jax import lax
from jax.experimental import pallas as pl
from jax.experimental.pallas import tpu as pltpu
from jax.sharding import PartitionSpec as P

MESH = pl.DeviceIdType.MESH
FAR_BELOW = -1e30
L = 128
NT = (((1,), (1,)), ((), ()))
TN = (((0,), (0,)), ((), ()))
NN = (((1,), (0,)), ((), ()))
BF = jnp.bfloat16
F32 = jnp.float32


def matmul(a, b, dims):
    return lax.dot_general(a, b, dims, preferred_element_type=F32)


def iota(shape, dim):
    return lax.broadcasted_iota(jnp.int32, shape, dim)


class Sizes:
    def __init__(self, vocab, rows, th, thead, dhead):
        self.V, self.X = vocab, rows
        self.Z = self.Y = math.isqrt(vocab // 2)
        self.R0, self.F = th
        self.G = self.R0 * self.Z
        self.nk = self.G // self.R0
        self.W = self.F // self.nk
        self.H = self.F // 2
        self.W2 = self.H // self.nk
        self.VT, self.VD = thead[0], dhead[0]
        self.ROWS = self.R0 * vocab
        self.CH = self.ROWS // rows
        self.SPC = self.CH // self.G


def body(
    s,
    th, dh, thead_hbm, dhead_hbm, dmap, dvalid, scale,
    loss_out, gh_out, ghead_out,
    thead, dhead, stage, stage_big, t0, d0, a_t, a_d, map_own, map_in, sel,
    tp, tr, dfull, dp, dr, ld, s_out, s_in, st_own, st_in, f0, f1, f2, c0, c1, c2,
    ga_t, ga_d, keep_t, keep_d, js_t, js_d, jr_t, jr_d, q_t, q_d, qr_t, qr_d,
    w_out, w_in, ghead,
    sem_head, sem_l1s, sem_l1r, sem_rs, sem_rr, sem_sibs, sem_sibr, sem_ms, sem_mr,
    sem_ts, sem_tr, sem_ds, sem_dr, sem_ss, sem_sr, sem_fs, sem_fr, sem_cs, sem_cr,
    sem_gs, sem_gr, sem_js, sem_jr, sem_qs, sem_qr, sem_ws, sem_wr, sem_out,
):
    V, X, Z, Y, R0, G, nk, W, H, W2 = s.V, s.X, s.Z, s.Y, s.R0, s.G, s.nk, s.W, s.H, s.W2
    v = lax.axis_index("vocab")
    x = lax.axis_index("rows")
    c = lax.rem(v, 2)
    chip = lax.div(v, 2)
    y = lax.rem(chip, Y)
    z = lax.div(chip, Y)
    sib = v + 1 - 2 * c

    def at(zz, yy, cc):
        return (zz * Y + yy) * 2 + cc

    def y_peer(k):
        return at(z, lax.rem(y + k, Y), c)

    def z_peer(k):
        return at(lax.rem(z + k, Z), y, c)

    def x_peer(k):
        return lax.rem(x + k, X)

    def rcopy(src, dst, ssem, rsem, vv, xx):
        return pltpu.make_async_remote_copy(
            src_ref=src, dst_ref=dst, send_sem=ssem, recv_sem=rsem,
            device_id=(vv, xx), device_id_type=MESH,
        )

    sends = []

    def send(src, dst, ssem, rsem, vv, xx=None):
        cp = rcopy(src, dst, ssem, rsem, vv, x if xx is None else xx)
        cp.start()
        sends.append(cp)

    def arrived(dst, rsem):
        rcopy(dst, dst, rsem, rsem, sib, x).wait_recv()

    load_t = pltpu.make_async_copy(thead_hbm, thead, sem_head.at[0])
    load_d = pltpu.make_async_copy(dhead_hbm, dhead, sem_head.at[1])
    load_t.start()
    load_d.start()

    owner = v < V // 2
    owner_of = lax.div(v, 2)

    barrier = pltpu.get_barrier_semaphore()

    def hello(vv, xx):
        pl.semaphore_signal(barrier, inc=1, device_id=(vv, xx), device_id_type=MESH)

    for k in range(1, Y):
        hello(y_peer(k), x)
    for k in range(1, Z):
        hello(z_peer(k), x)
    hello(sib, x)
    for k in range(1, X):
        hello(v, x_peer(k))

    @pl.when(v > 0)
    def _():
        hello(owner_of, x)

    @pl.when(owner)
    def _():
        hello(2 * v + 1, x)

    @pl.when(jnp.logical_and(owner, v > 0))
    def _():
        hello(2 * v, x)

    for ref, dst, slot in ((th, t0, y), (dh, d0, z)):
        for k in range(nk):
            for a in range(W // L):
                cols = slice(k * W + a * L, k * W + (a + 1) * L)
                stage[a, pl.ds(k, R0, stride=nk), :] = ref[:, cols].astype(F32)
        for a in range(W // L):
            dst[slot, :, a * L:(a + 1) * L] = stage[a].astype(BF)
    masked_map = jnp.where(dvalid[...] > 0, dmap[...], -1)
    map_own[...] = jnp.broadcast_to(masked_map, map_own.shape)

    live_owner = owner.astype(jnp.int32)
    live_v = (v > 0).astype(jnp.int32)
    pl.semaphore_wait(
        barrier, (Y - 1) + (Z - 1) + 1 + (X - 1) + live_v + live_owner * (1 + live_v)
    )

    for k in range(1, Y):
        send(t0.at[y], t0.at[y], sem_l1s.at[0, k], sem_l1r.at[0, k], y_peer(k))
        send(d0.at[z], d0.at[z], sem_l1s.at[1, k], sem_l1r.at[1, k], z_peer(k))

    @pl.when(v > 0)
    def _():
        rcopy(map_own, map_in.at[c], sem_ms, sem_mr.at[c], owner_of, x).start()

    @pl.when(v == 0)
    def _():
        map_in[0] = map_own[...]

    def relayout(src, dst, slot):
        for i in range(Y):
            for a in range(W // L):
                stage_big[a, i * G:(i + 1) * G, :] = src[i, :, a * L:(a + 1) * L].astype(F32)
        for k in range(nk):
            for a in range(W // L):
                cols = slice(k * W + a * L, k * W + (a + 1) * L)
                dst[slot, :, cols] = stage_big[a, pl.ds(k, G, stride=nk), :].astype(BF)

    for k in range(1, Y):
        arrived(t0.at[lax.rem(y + Y - k, Y)], sem_l1r.at[0, k])
    relayout(t0, a_t, z * 2 + c)

    half = Z // 2

    def ring_slot(q, n):
        return lax.rem(q + 2 * n, n) * 2 + c

    rings = (
        (0, a_t, z, Z, z_peer),
        (1, a_d, y, Y, y_peer),
    )

    def part(buf, slot, direction, step):
        if step < half:
            return buf.at[slot]
        return buf.at[slot, :, pl.ds(0, H)] if direction == 0 else buf.at[slot, :, pl.ds(H, H)]

    def ring_send(ring, step):
        i, buf, pos, n, peer = rings[ring]
        for direction in (0, 1):
            q = pos - step + 1 if direction == 0 else pos + step - 1
            ref = part(buf, ring_slot(q, n), direction, step)
            send(
                ref, ref, sem_rs.at[i, direction, step - 1], sem_rr.at[i, direction, step - 1],
                peer(1 if direction == 0 else n - 1),
            )

    def ring_wait(ring, step):
        i, buf, pos, n, _ = rings[ring]
        for direction in (0, 1):
            q = pos - step if direction == 0 else pos + step
            arrived(
                part(buf, ring_slot(q, n), direction, step), sem_rr.at[i, direction, step - 1]
            )

    def sib_refs(ring, step, core):
        i, buf, pos, n, _ = rings[ring]
        if step == 0:
            return [(buf.at[lax.rem(pos, n) * 2 + core], 0)]
        if step == half:
            return [(buf.at[lax.rem(pos + half, n) * 2 + core], 2 * half - 1)]
        return [
            (buf.at[lax.rem(pos - step + n, n) * 2 + core], 2 * step - 1),
            (buf.at[lax.rem(pos + step, n) * 2 + core], 2 * step),
        ]

    def sib_send(ring, step):
        for ref, k in sib_refs(ring, step, c):
            send(ref, ref, sem_sibs.at[ring, k], sem_sibr.at[ring, k], sib)

    def sib_wait(ring, step):
        for ref, k in sib_refs(ring, step, 1 - c):
            arrived(ref, sem_sibr.at[ring, k])

    ring_send(0, 1)
    sib_send(0, 0)
    for k in range(1, Z):
        arrived(d0.at[lax.rem(z + Z - k, Z)], sem_l1r.at[1, k])
    relayout(d0, a_d, y * 2 + c)
    ring_send(1, 1)
    sib_send(1, 0)

    @pl.when(v > 0)
    def _():
        rcopy(map_own, map_in.at[c], sem_ms, sem_mr.at[c], owner_of, x).wait_send()

    @pl.when(owner)
    def _():
        arrived(map_in.at[1], sem_mr.at[1])

        @pl.when(v > 0)
        def _():
            arrived(map_in.at[0], sem_mr.at[0])

        ids = iota((s.VT, s.VD), 0) + v * s.VT
        for i in range(2):
            hit = ids == jnp.broadcast_to(map_in[i, 0:1, :], (s.VT, s.VD))
            sel[:, i * s.VD:(i + 1) * s.VD] = jnp.where(hit, 1.0, 0.0).astype(BF)

    load_t.wait()

    def target_chunk(r):
        block = a_t[pl.ds(r * s.SPC, s.SPC)].reshape(s.CH, s.F)
        tp[r] = matmul(block, thead[...], NT)
        k = lax.rem(x - r + X, X)

        @pl.when(r != x)
        def _():
            rcopy(tp.at[r], tr.at[k], sem_ts.at[k], sem_tr.at[k], v, r).start()

    own = lax.div(z * 2, s.SPC)
    if X == 4 and Z == 8:
        sign = 1 - 2 * lax.rem(z, 2)
        order = [(1, own), (2, lax.rem(own - sign + X, X)), (3, lax.rem(own + sign + X, X)),
                 (4, lax.rem(own + 2, X))]
    else:
        order = [(half, lax.rem(own + k, X)) for k in range(X)]
    for step in range(0, half + 1):
        if step > 0:
            for ring in (0, 1):
                ring_wait(ring, step)
                if step < half:
                    ring_send(ring, step + 1)
                sib_send(ring, step)
        sib_wait(0, step)
        for when_, r in order:
            if when_ == step:
                target_chunk(r)
        sib_wait(1, step)

    load_d.wait()
    d_part = matmul(a_d[...].reshape(s.ROWS, s.F), dhead[...], NT)
    for a in range(s.VD // L):
        dfull[a] = d_part[:, a * L:(a + 1) * L]
    zpx = Z // X
    for zz in range(Z):
        for cc in range(2):
            for j in range(R0):
                to = pl.ds(((zz % zpx) * 2 + cc) * G + j, Y, stride=R0)
                for a in range(s.VD // L):
                    dp[zz // zpx, a, to, :] = dfull[
                        a, pl.ds((cc * Z + zz) * R0 + j, Y, stride=2 * G), :
                    ]
    for k in range(1, X):
        send(dp.at[lax.rem(x - k + X, X)], dr.at[k], sem_ds.at[k], sem_dr.at[k], v,
             lax.rem(x - k + X, X))

    for k in range(1, X):
        arrived(tr.at[k], sem_tr.at[k])
    lt = tp[x]
    for k in range(1, X):
        lt = lt + tr[k]
    live_limit = s.VT * V - s.VT // 2
    live = iota((1, s.VT), 1) + v * s.VT < live_limit
    tm = jnp.max(jnp.where(live, lt, FAR_BELOW), axis=1, keepdims=True)
    te = jnp.where(live, jnp.exp(lt - tm), 0.0)
    ts = jnp.sum(te, axis=1, keepdims=True)

    s_out[...] = jnp.zeros_like(s_out)

    @pl.when(owner)
    def _():
        te16 = te.astype(BF)
        for i in range(2):
            s_out[i] = matmul(te16, sel[:, i * s.VD:(i + 1) * s.VD], NN).astype(BF)

    mass_here = jnp.sum(s_out[0].astype(F32) + s_out[1].astype(F32), axis=1, keepdims=True)

    eye = iota((s.CH, 128), 0) == iota((s.CH, 128), 1)

    def to_row(col):
        return jnp.sum(jnp.where(eye, col, 0.0), axis=0, keepdims=True)

    def to_col(row):
        return jnp.sum(jnp.where(eye, row, 0.0), axis=1, keepdims=True)

    st_own[...] = jnp.broadcast_to(to_row(tm), st_own.shape)

    @pl.when(owner)
    def _():
        rcopy(s_out.at[1], s_in, sem_ss.at[1], sem_sr.at[0], 2 * v + 1, x).start()
        rcopy(st_own, st_in, sem_ss.at[3], sem_sr.at[1], 2 * v + 1, x).start()

        @pl.when(v > 0)
        def _():
            rcopy(s_out.at[0], s_in, sem_ss.at[0], sem_sr.at[0], 2 * v, x).start()
            rcopy(st_own, st_in, sem_ss.at[2], sem_sr.at[1], 2 * v, x).start()

        @pl.when(v == 0)
        def _():
            s_in[...] = s_out[0]
            st_in[...] = st_own[...]

    valid = dvalid[...] > 0
    for k in range(1, X):
        arrived(dr.at[k], sem_dr.at[k])
    l_d = dp[x]
    for k in range(1, X):
        l_d = l_d + dr[k]
    l_d = jnp.concatenate([l_d[a] for a in range(s.VD // L)], axis=1)
    ld[...] = l_d
    dm = jnp.max(jnp.where(valid, l_d, FAR_BELOW), axis=1, keepdims=True)
    ds = jnp.sum(jnp.where(valid, jnp.exp(l_d - dm), 0.0), axis=1, keepdims=True)

    zero_row = jnp.zeros((5, 128), F32)
    tmr = to_row(tm)
    maxes = jnp.concatenate([tmr, tmr, to_row(dm), zero_row], axis=0)
    sums = jnp.concatenate([to_row(ts), to_row(mass_here), to_row(ds), zero_row], axis=0)

    def exchange(buf, slot, n, peer, ssem, rsem):
        for k in range(1, n):
            send(buf.at[slot], buf.at[slot], ssem.at[k], rsem.at[k], peer(k))

    def exchange_wait(buf, slot, n, rsem):
        for k in range(1, n):
            arrived(buf.at[lax.rem(slot + n - k, n)], rsem.at[k])

    hops = (
        (f0, c0, c, 2, lambda k: sib),
        (f1, c1, y, Y, y_peer),
        (f2, c2, z, Z, z_peer),
    )
    for h, (buf, _, slot, n, peer) in enumerate(hops):
        buf[slot, 0] = maxes
        buf[slot, 1] = sums
        exchange(buf, slot, n, peer, sem_fs.at[h], sem_fr.at[h])
        exchange_wait(buf, slot, n, sem_fr.at[h])
        maxes = buf[0, 0]
        for i in range(1, n):
            maxes = jnp.maximum(maxes, buf[i, 0])
        sums = buf[0, 1] * jnp.exp(buf[0, 0] - maxes)
        for i in range(1, n):
            sums = sums + buf[i, 1] * jnp.exp(buf[i, 0] - maxes)

    @pl.when(v > 0)
    def _():
        arrived(s_in, sem_sr.at[0])
        arrived(st_in, sem_sr.at[1])

    t_max, t_total = maxes[0:1], sums[0:1]
    factor = to_col(jnp.exp(st_in[0:1] - t_max) / t_total)
    mass = to_col(sums[1:2] / t_total)
    lse = to_col(maxes[2:3] + jnp.log(sums[2:3]))
    soft = s_in[...].astype(F32) * factor
    l_d = ld[...]
    grad = scale[0, 0] * (jnp.exp(l_d - lse) * mass - soft)
    ga_t[pl.ds(x * s.SPC, s.SPC)] = (
        jnp.where(valid, grad, 0.0).astype(BF).reshape(s.SPC, G, s.VD)
    )
    for k in range(1, X):
        chunk = ga_t.at[pl.ds(x * s.SPC, s.SPC)]
        send(chunk, chunk, sem_gs.at[k], sem_gr.at[k], v, x_peer(k))

    cross = jnp.broadcast_to(to_row(jnp.sum(soft * l_d, axis=1, keepdims=True)), (8, 128))

    def cross_send(h, value):
        _, buf, slot, n, peer = hops[h]
        buf[slot] = value
        exchange(buf, slot, n, peer, sem_cs.at[h], sem_cr.at[h])

    def cross_wait(h):
        _, buf, slot, n, _ = hops[h]
        exchange_wait(buf, slot, n, sem_cr.at[h])
        total = buf[0]
        for i in range(1, n):
            total = total + buf[i]
        return total

    cross_send(0, cross)
    shape = (s.ROWS, s.ROWS)
    dpos, tpos = iota(shape, 0), iota(shape, 1)
    lr, lz = R0.bit_length() - 1, Z.bit_length() - 1
    dj = dpos & (R0 - 1)
    dz = (dpos >> lr) & (Z - 1)
    dc = (dpos >> (lr + lz)) & 1
    dy = dpos >> (lr + lz + 1)
    perm = jnp.where((((dz * 2 + dc) * Y + dy) << lr) + dj == tpos, 1.0, 0.0).astype(BF)

    cross_send(1, cross_wait(0))

    for k in range(1, X):
        other = ga_t.at[pl.ds(lax.rem(x + X - k, X) * s.SPC, s.SPC)]
        arrived(other, sem_gr.at[k])
    ga_d[...] = (
        matmul(perm, ga_t[...].reshape(s.ROWS, s.VD), NN).astype(BF).reshape(2 * Y, G, s.VD)
    )

    def rows_of(buf, core):
        return jnp.concatenate([buf[i * 2 + core] for i in range(Z)], axis=0)

    js_t[...] = matmul(rows_of(ga_t, 1 - c), dhead[:, :H], NN).astype(BF).reshape(Z, G, H)
    send(js_t, jr_t, sem_js.at[0], sem_jr.at[0], sib)
    js_d[...] = matmul(rows_of(ga_d, 1 - c), dhead[:, H:], NN).astype(BF).reshape(Y, G, H)
    send(js_d, jr_d, sem_js.at[1], sem_jr.at[1], sib)
    keep_t[...] = matmul(rows_of(ga_t, c), dhead[:, :H], NN).reshape(Z, G, H)
    keep_d[...] = matmul(rows_of(ga_d, c), dhead[:, H:], NN).reshape(Y, G, H)

    parts = (
        (0, jr_t, keep_t, q_t, qr_t, z, Z, z_peer, y, Y, y_peer),
        (1, jr_d, keep_d, q_d, qr_d, y, Y, y_peer, z, Z, z_peer),
    )
    for i, jr, keep, q, qr, pos, n, peer, _, _, _ in parts:
        arrived(jr, sem_jr.at[i])
        for k in range(1, n):
            to = lax.rem(pos + k, n)
            q[k] = (keep[to] + jr[to].astype(F32)).astype(BF)
            send(q.at[k], qr.at[k], sem_qs.at[i, k], sem_qr.at[i, k], peer(k))

    ghead[...] = matmul(ga_d[...].reshape(s.ROWS, s.VD), a_d[...].reshape(s.ROWS, s.F), TN).astype(
        BF
    )
    store = pltpu.make_async_copy(ghead, ghead_out, sem_out)
    store.start()

    cross_send(2, cross_wait(1))

    for i, jr, keep, q, qr, pos, n, peer, pos2, n2, peer2 in parts:
        total = keep[pos] + jr[pos].astype(F32)
        for k in range(1, n):
            arrived(qr.at[k], sem_qr.at[i, k])
            total = total + qr[k].astype(F32)
        for k in range(nk):
            stage_big[0, pl.ds(k, G, stride=nk), :] = total[:, k * W2:(k + 1) * W2]
        for p in range(n2):
            w_out[i, p] = stage_big[0, p * G:(p + 1) * G, :].astype(BF)
        for k in range(1, n2):
            send(
                w_out.at[i, lax.rem(pos2 + k, n2)], w_in.at[i, k],
                sem_ws.at[i, k], sem_wr.at[i, k], peer2(k),
            )
        w_in[i, 0] = w_out[i, pos2]

    total_cross = to_col(cross_wait(2)[0:1])
    loss = mass * lse - total_cross
    shape = (s.CH, 128)
    src, dst = iota(shape, 0), iota(shape, 1)
    sj = src & (R0 - 1)
    sy = (src >> lr) & (Y - 1)
    sc = (src >> (lr + lz)) & 1
    sz = src >> (lr + lz + 1)
    place = (((sz * Y + sy) * 2 + sc) << lr) + sj == dst
    loss_out[...] = jnp.sum(jnp.where(place, loss, 0.0), axis=0, keepdims=True)

    for i, jr, keep, q, qr, pos, n, peer, pos2, n2, peer2 in parts:
        total = w_in[i, 0].astype(F32)
        for k in range(1, n2):
            arrived(w_in.at[i, k], sem_wr.at[i, k])
            total = total + w_in[i, k].astype(F32)
        stage[0] = total
        for k in range(nk):
            gh_out[:, i * H + k * W2:i * H + (k + 1) * W2] = stage[
                0, pl.ds(k, R0, stride=nk), :
            ].astype(BF)

    for cp in sends:
        cp.wait_send()
    for k in range(1, X):
        rcopy(tr.at[k], tr.at[k], sem_ts.at[k], sem_ts.at[k], v, x).wait_send()

    @pl.when(owner)
    def _():
        rcopy(s_out.at[1], s_in, sem_ss.at[1], sem_sr.at[0], 2 * v + 1, x).wait_send()
        rcopy(st_own, st_in, sem_ss.at[3], sem_sr.at[1], 2 * v + 1, x).wait_send()

        @pl.when(v > 0)
        def _():
            rcopy(s_out.at[0], s_in, sem_ss.at[0], sem_sr.at[0], 2 * v, x).wait_send()
            rcopy(st_own, st_in, sem_ss.at[2], sem_sr.at[1], 2 * v, x).wait_send()

    store.wait()


def on_device(vocab, rows, th, thead, dh, dhead, dmap, dvalid, scale):
    s = Sizes(vocab, rows, th.shape, thead.shape, dhead.shape)
    Z, Y, X, G, F, H, W, W2, VT, VD, CH = (
        s.Z, s.Y, s.X, s.G, s.F, s.H, s.W, s.W2, s.VT, s.VD, s.CH
    )
    vm = pltpu.VMEM
    dma = pltpu.SemaphoreType.DMA
    scratch = [
        vm((VT, F), BF), vm((VD, F), BF),
        vm((W // L, G, L), F32), vm((W // L, G * Y, L), F32),
        vm((Y, G, W), BF), vm((Z, G, W), BF),
        vm((2 * Z, G, F), BF), vm((2 * Y, G, F), BF),
        vm((8, VD), jnp.int32), vm((2, 8, VD), jnp.int32),
        vm((VT, 2 * VD), BF),
        vm((X, CH, VT), F32), vm((X, CH, VT), F32),
        vm((VD // L, s.ROWS, L), F32),
        vm((X, VD // L, CH, L), F32), vm((X, VD // L, CH, L), F32),
        vm((CH, VD), F32),
        vm((2, CH, VD), BF), vm((CH, VD), BF),
        vm((8, 128), F32), vm((8, 128), F32),
        vm((2, 2, 8, 128), F32), vm((Y, 2, 8, 128), F32), vm((Z, 2, 8, 128), F32),
        vm((2, 8, 128), F32), vm((Y, 8, 128), F32), vm((Z, 8, 128), F32),
        vm((2 * Z, G, VD), BF), vm((2 * Y, G, VD), BF),
        vm((Z, G, H), F32), vm((Y, G, H), F32),
        vm((Z, G, H), BF), vm((Y, G, H), BF),
        vm((Z, G, H), BF), vm((Y, G, H), BF),
        vm((Z, G, H), BF), vm((Y, G, H), BF),
        vm((Z, G, H), BF), vm((Y, G, H), BF),
        vm((2, Y, G, W2), BF), vm((2, Y, G, W2), BF),
        vm((VD, F), BF),
        dma((2,)),
        dma((2, Y)), dma((2, Y)),
        dma((2, 2, Z // 2)), dma((2, 2, Z // 2)),
        dma((2, Z)), dma((2, Z)),
        dma, dma((2,)),
        dma((X,)), dma((X,)), dma((X,)), dma((X,)),
        dma((4,)), dma((2,)),
        dma((3, Z)), dma((3, Z)), dma((3, Z)), dma((3, Z)),
        dma((X,)), dma((X,)),
        dma((2,)), dma((2,)), dma((2, Z)), dma((2, Z)), dma((2, Z)), dma((2, Z)),
        dma,
    ]
    any_ = pl.BlockSpec(memory_space=pl.ANY)
    vmem = pl.BlockSpec(memory_space=pltpu.VMEM)
    smem = pl.BlockSpec(memory_space=pltpu.SMEM)
    loss, gh, ghead = pl.pallas_call(
        functools.partial(body, s),
        out_shape=(
            jax.ShapeDtypeStruct((1, 128), F32),
            jax.ShapeDtypeStruct((s.R0, F), BF),
            jax.ShapeDtypeStruct((VD, F), BF),
        ),
        in_specs=[vmem, vmem, any_, any_, vmem, vmem, smem],
        out_specs=(vmem, vmem, any_),
        scratch_shapes=scratch,
        compiler_params=pltpu.CompilerParams(
            collective_id=0, has_side_effects=True, vmem_limit_bytes=48 * 1024 * 1024
        ),
    )(th, dh, thead, dhead, dmap.reshape(1, VD), dvalid.reshape(1, VD), scale.reshape(1, 1))
    return loss[0, :CH], gh, ghead


def solution(mesh):
    both, one = P("vocab", "rows"), P("vocab")
    return jax.shard_map(
        functools.partial(on_device, mesh.shape["vocab"], mesh.shape["rows"]),
        mesh=mesh,
        in_specs=(both, both, both, both, one, one, P()),
        out_specs=(P("rows"), both, both),
        check_vma=False,
    )
```

time: 1610 us -> 91.4 us (0.06)
  blocking collectives: 1300 us -> 0 us
  waiting for transfers between devices: 254 us -> 0 us
  Pallas kernels: 0 us -> 82 us
    psum x3 -> x0, blocking collectives: 1010 us -> none  [the longest x2 762 us: on_device(): lax.psum((jnp.sum(soft_wide, axis=1), jnp.sum(soft_wide * draft_logits, a...]
    pmax x1 -> x0, blocking collectives: 250 us -> none  [on_device(): target_max, draft_max = lax.pmax((target_local, draft_local), 'vocab')]
    all_gather x3 -> x0, waiting for transfers between devices: 207 us -> none  [the longest x1 77.3 us: on_device(): incoming = lax.all_gather(outgoing, 'vocab', axis=1, tiled=True)]
    pallas_call x0 -> x1, Pallas kernels: none -> 82 us  [on_device(): pl.pallas_call(functools.partial(body, s), out_shape=(jax.ShapeDtypeStruc...]
    reduce_scatter x2 -> x0, waiting for transfers between devices: 45.5 us -> none  [the longest x1 29.5 us: on_device(): lax.psum_scatter(target_part, 'rows', scatter_dimension=0, tiled=True)]
    unnamed x1 -> x0, blocking collectives: 27.8 us -> none
  transfers between devices with their start and end apart: 5 -> 0, of which waited for: 5 -> 0; matrix products, arithmetic and copies ran while one was open for 1% -> 0% of each run, Pallas kernels for 0% -> 0%
where the time goes in v1:
time: 91.4 us; the launch traced here: 91.1 us
  Pallas kernels  82 us (90%)
  local copies, waits for them, and re-layouts  7.79 us (9%)
  between operations  1.3 us (1%)
    pallas_call x1, Pallas kernels, on_device(): pl.pallas_call(functools.partial(body, s), out_shape=(jax.ShapeDtypeStruc...  82 us
    unnamed x14, local copies, waits for them, and re-layouts  7.27 us

profile of v1, /device:TPU:1, one launch (start us, length us, event | category | flops | bytes accessed | tf_op | source)
XLA Modules:
  0.0 91.1 jit_solution(1432279880469174565)
XLA Ops:
  1.3 0.0 copy-start
  1.3 1.7 %copy-done = bf16[640,2048]{1,0:T(8,128)(2,1)S(1)} copy-done((bf16[640,2048]{1,0:T(8,128)(2,1)S(1)}, bf16[640,2048]{1,0:T(8,128)(2,1)}, u32[]{:S(2)}) %copy-start) | copy-done | bytes 2621464
  3.0 0.0 copy-start.1
  3.0 1.2 %copy-done.1 = bf16[256,2048]{1,0:T(8,128)(2,1)S(1)} copy-done((bf16[256,2048]{1,0:T(8,128)(2,1)S(1)}, bf16[256,2048]{1,0:T(8,128)(2,1)}, u32[]{:S(2)}) %copy-start.1) | copy-done | bytes 1048600
  4.2 0.0 copy-start.2
  4.2 0.7 copy-done.2
  4.9 0.0 copy-start.3
  4.9 0.7 copy-done.3
  5.6 0.0 copy-start.4
  5.6 0.7 copy-done.4
  6.3 0.0 copy-start.5
  6.3 0.7 copy-done.5
  7.0 82.0 %shard_map.94 = (f32[1,128]{1,0:T(1,128)S(1)}, bf16[2,2048]{1,0:T(2,128)(2,1)S(1)}, bf16[256,2048]{1,0:T(8,128)(2,1)S(1)}) custom-call(bf16[2,2048]{1,0:T(2,128)(2,1)S(1)} %copy-done.2, bf16[2,2048]{1,0:T(2,128)(2,1)S(1)} %copy-done.3, bf16[640,2048]{1,0:T(8,128)(2,1)S(1)} %copy-done, bf16[256,2048]{1,0:T(8,128)(2,1)S(1)} %copy-done.1, ...), custom_call_target="tpu_custom_call" | custom-call | tf_op jit(solution)/shard_map/pallas_call | solution.py:563
  89.0 0.5 slice_bitcast_fusion
  89.5 0.6 copy.13
  90.1 1.0 %copy.14 = bf16[256,2048]{1,0:T(8,128)(2,1)} copy(bf16[256,2048]{1,0:T(8,128)(2,1)S(1)} %get-tuple-element.14) | data formatting | bytes 2097152
Async XLA Ops:
  1.3 1.7 %copy-start = (bf16[640,2048]{1,0:T(8,128)(2,1)S(1)}, bf16[640,2048]{1,0:T(8,128)(2,1)}, u32[]{:S(2)}) copy-start(bf16[640,2048]{1,0:T(8,128)(2,1)} %thead_hbm.1) | copy-start | bytes 7864324
  3.0 1.2 %copy-start.1 = (bf16[256,2048]{1,0:T(8,128)(2,1)S(1)}, bf16[256,2048]{1,0:T(8,128)(2,1)}, u32[]{:S(2)}) copy-start(bf16[256,2048]{1,0:T(8,128)(2,1)} %dhead_hbm.1) | copy-start | bytes 3145732
  4.2 0.7 copy-start.2
  4.9 0.7 copy-start.3
  5.6 0.7 copy-start.4
  6.3 0.7 copy-start.5

commit v2 on v1

--- a/solution.py
+++ b/solution.py
@@ -44,10 +44,10 @@
 
 def body(
     s,
-    th, dh, thead_hbm, dhead_hbm, dmap, dvalid, scale,
+    th_hbm, dh_hbm, thead_hbm, dhead_hbm, dmap_hbm, dvalid_hbm, scale,
     loss_out, gh_out, ghead_out,
-    thead, dhead, stage, stage_big, t0, d0, a_t, a_d, map_own, map_in, sel,
-    tp, tr, dfull, dp, dr, ld, s_out, s_in, st_own, st_in, f0, f1, f2, c0, c1, c2,
+    th, dh, dmap, dvalid, thead, dhead, stage, stage_big, t0, d0, a_t, a_d, map_own, map_in, sel,
+    tp0, tp1, tp2, tr0, tr1, tr2, tfull, dp, dr, ld, s_out, s_in, st_own, st_in, f0, f1, f2, c0, c1, c2,
     ga_t, ga_d, keep_t, keep_d, js_t, js_d, jr_t, jr_d, q_t, q_d, qr_t, qr_d,
     w_out, w_in, ghead,
     sem_head, sem_l1s, sem_l1r, sem_rs, sem_rr, sem_sibs, sem_sibr, sem_ms, sem_mr,
@@ -81,7 +81,9 @@
             device_id=(vv, xx), device_id_type=MESH,
         )
 
+    tp, tr = (tp0, tp1, tp2), (tr0, tr1, tr2)
     sends = []
+    drains = []
 
     def send(src, dst, ssem, rsem, vv, xx=None):
         cp = rcopy(src, dst, ssem, rsem, vv, x if xx is None else xx)
@@ -91,6 +93,20 @@
     def arrived(dst, rsem):
         rcopy(dst, dst, rsem, rsem, sib, x).wait_recv()
 
+    def finish():
+        for cp in sends:
+            cp.wait_send()
+        for drain in drains:
+            drain()
+
+    small = [
+        pltpu.make_async_copy(src, dst, sem_head.at[2 + i])
+        for i, (src, dst) in enumerate(
+            ((th_hbm, th), (dh_hbm, dh), (dmap_hbm, dmap), (dvalid_hbm, dvalid))
+        )
+    ]
+    for cp in small:
+        cp.start()
     load_t = pltpu.make_async_copy(thead_hbm, thead, sem_head.at[0])
     load_d = pltpu.make_async_copy(dhead_hbm, dhead, sem_head.at[1])
     load_t.start()
@@ -124,7 +140,10 @@
     def _():
         hello(2 * v, x)
 
-    for ref, dst, slot in ((th, t0, y), (dh, d0, z)):
+    for cp in small:
+        cp.wait()
+
+    for ref, dst, slot in ((th, t0, z), (dh, d0, y)):
         for k in range(nk):
             for a in range(W // L):
                 cols = slice(k * W + a * L, k * W + (a + 1) * L)
@@ -140,13 +159,20 @@
         barrier, (Y - 1) + (Z - 1) + 1 + (X - 1) + live_v + live_owner * (1 + live_v)
     )
 
-    for k in range(1, Y):
-        send(t0.at[y], t0.at[y], sem_l1s.at[0, k], sem_l1r.at[0, k], y_peer(k))
-        send(d0.at[z], d0.at[z], sem_l1s.at[1, k], sem_l1r.at[1, k], z_peer(k))
+    for k in range(1, Z):
+        send(t0.at[z], t0.at[z], sem_l1s.at[0, k], sem_l1r.at[0, k], z_peer(k))
+        send(d0.at[y], d0.at[y], sem_l1s.at[1, k], sem_l1r.at[1, k], y_peer(k))
 
     @pl.when(v > 0)
     def _():
         rcopy(map_own, map_in.at[c], sem_ms, sem_mr.at[c], owner_of, x).start()
+
+    def drain_map():
+        @pl.when(v > 0)
+        def _():
+            rcopy(map_own, map_in.at[c], sem_ms, sem_mr.at[c], owner_of, x).wait_send()
+
+    drains.append(drain_map)
 
     @pl.when(v == 0)
     def _():
@@ -161,73 +187,63 @@
                 cols = slice(k * W + a * L, k * W + (a + 1) * L)
                 dst[slot, :, cols] = stage_big[a, pl.ds(k, G, stride=nk), :].astype(BF)
 
+    for k in range(1, Z):
+        arrived(t0.at[lax.rem(z + Z - k, Z)], sem_l1r.at[0, k])
+    relayout(t0, a_t, 0)
+
+    hop = (2, -2, 1, -1, 1, -1, 2, -2)
+    held = (0, 0, 0, 0, -2, 2, -2, 2)
+    if Z == 8:
+        first_kinds, next_kinds = (0, 1, 2, 3), {0: (4, 6), 1: (5, 7)}
+        turns, stages = (0, -2, 2, -1, 1, -3, 3, 4), (0, 5, 7, 8)
+    else:
+        first_kinds, next_kinds = (2,), {}
+        turns, stages = (0, 1), (0, 2)
+
+    def turn_slot(ring, turn, core):
+        if ring == 1:
+            return lax.rem(z + turn + Z, Z) * 2 + core
+        near = [i for i, other in enumerate(turns) if (other - turn) % Y == 0]
+        return near[0] * 2 + (0 if core is c else 1)
+
+    def block_of(ring, turn, kind, core):
+        buf, slot = (a_t, a_d)[ring], turn_slot(ring, turn, core)
+        if kind is None or kind < 6:
+            return buf.at[slot]
+        return buf.at[slot, :, pl.ds(0, H)] if kind == 6 else buf.at[slot, :, pl.ds(H, H)]
+
+    def ring_send(ring, kind):
+        src = block_of(ring, held[kind], kind, c)
+        dst = src if ring == 1 else block_of(ring, held[kind] - hop[kind], kind, c)
+        send(src, dst, sem_rs.at[ring, kind], sem_rr.at[ring, kind],
+             (y_peer, z_peer)[ring](hop[kind] % Z))
+
+    def ring_wait(ring, kind):
+        arrived(block_of(ring, held[kind] - hop[kind], kind, c), sem_rr.at[ring, kind])
+
+    def sib_turn(kind):
+        return 0 if kind is None else held[kind] - hop[kind]
+
+    def sib_send(ring, kind):
+        turn, k = sib_turn(kind), 7 if kind is None else kind
+        src = block_of(ring, turn, None, c)
+        dst = src if ring == 1 else block_of(ring, turn, None, 1 - c)
+        send(src, dst, sem_sibs.at[ring, k], sem_sibr.at[ring, k], sib)
+
+    def sib_wait(ring, kind):
+        k = 7 if kind is None else kind
+        arrived(block_of(ring, sib_turn(kind), None, 1 - c), sem_sibr.at[ring, k])
+
+    def ring_start(ring):
+        for kind in first_kinds:
+            ring_send(ring, kind)
+        sib_send(ring, None)
+
+    ring_start(0)
     for k in range(1, Y):
-        arrived(t0.at[lax.rem(y + Y - k, Y)], sem_l1r.at[0, k])
-    relayout(t0, a_t, z * 2 + c)
-
-    half = Z // 2
-
-    def ring_slot(q, n):
-        return lax.rem(q + 2 * n, n) * 2 + c
-
-    rings = (
-        (0, a_t, z, Z, z_peer),
-        (1, a_d, y, Y, y_peer),
-    )
-
-    def part(buf, slot, direction, step):
-        if step < half:
-            return buf.at[slot]
-        return buf.at[slot, :, pl.ds(0, H)] if direction == 0 else buf.at[slot, :, pl.ds(H, H)]
-
-    def ring_send(ring, step):
-        i, buf, pos, n, peer = rings[ring]
-        for direction in (0, 1):
-            q = pos - step + 1 if direction == 0 else pos + step - 1
-            ref = part(buf, ring_slot(q, n), direction, step)
-            send(
-                ref, ref, sem_rs.at[i, direction, step - 1], sem_rr.at[i, direction, step - 1],
-                peer(1 if direction == 0 else n - 1),
-            )
-
-    def ring_wait(ring, step):
-        i, buf, pos, n, _ = rings[ring]
-        for direction in (0, 1):
-            q = pos - step if direction == 0 else pos + step
-            arrived(
-                part(buf, ring_slot(q, n), direction, step), sem_rr.at[i, direction, step - 1]
-            )
-
-    def sib_refs(ring, step, core):
-        i, buf, pos, n, _ = rings[ring]
-        if step == 0:
-            return [(buf.at[lax.rem(pos, n) * 2 + core], 0)]
-        if step == half:
-            return [(buf.at[lax.rem(pos + half, n) * 2 + core], 2 * half - 1)]
-        return [
-            (buf.at[lax.rem(pos - step + n, n) * 2 + core], 2 * step - 1),
-            (buf.at[lax.rem(pos + step, n) * 2 + core], 2 * step),
-        ]
-
-    def sib_send(ring, step):
-        for ref, k in sib_refs(ring, step, c):
-            send(ref, ref, sem_sibs.at[ring, k], sem_sibr.at[ring, k], sib)
-
-    def sib_wait(ring, step):
-        for ref, k in sib_refs(ring, step, 1 - c):
-            arrived(ref, sem_sibr.at[ring, k])
-
-    ring_send(0, 1)
-    sib_send(0, 0)
-    for k in range(1, Z):
-        arrived(d0.at[lax.rem(z + Z - k, Z)], sem_l1r.at[1, k])
-    relayout(d0, a_d, y * 2 + c)
-    ring_send(1, 1)
-    sib_send(1, 0)
-
-    @pl.when(v > 0)
-    def _():
-        rcopy(map_own, map_in.at[c], sem_ms, sem_mr.at[c], owner_of, x).wait_send()
+        arrived(d0.at[lax.rem(y + Y - k, Y)], sem_l1r.at[1, k])
+    relayout(d0, a_d, z * 2 + c)
+    ring_start(1)
 
     @pl.when(owner)
     def _():
@@ -244,57 +260,61 @@
 
     load_t.wait()
 
-    def target_chunk(r):
-        block = a_t[pl.ds(r * s.SPC, s.SPC)].reshape(s.CH, s.F)
-        tp[r] = matmul(block, thead[...], NT)
-        k = lax.rem(x - r + X, X)
-
-        @pl.when(r != x)
-        def _():
-            rcopy(tp.at[r], tr.at[k], sem_ts.at[k], sem_tr.at[k], v, r).start()
-
-    own = lax.div(z * 2, s.SPC)
-    if X == 4 and Z == 8:
-        sign = 1 - 2 * lax.rem(z, 2)
-        order = [(1, own), (2, lax.rem(own - sign + X, X)), (3, lax.rem(own + sign + X, X)),
-                 (4, lax.rem(own + 2, X))]
-    else:
-        order = [(half, lax.rem(own + k, X)) for k in range(X)]
-    for step in range(0, half + 1):
-        if step > 0:
+    zpx = Z // X
+    per = zpx * R0
+
+    def target_stage(st):
+        lo, hi = stages[st] * 2, stages[st + 1] * 2
+        tfull[lo * G:hi * G, :] = matmul(
+            a_t[lo:hi].reshape((hi - lo) * G, s.F), thead[...], NT
+        )
+        for b in range(lo, hi):
+            for r in range(X):
+                tp[st][r, (b - lo) * per:(b - lo + 1) * per, :] = tfull[
+                    b * G + r * per:b * G + (r + 1) * per, :
+                ]
+        for k in range(1, X):
+            to = lax.rem(x - k + X, X)
+            send(tp[st].at[to], tr[st].at[k], sem_ts.at[st, k], sem_tr.at[st, k], v, to)
+
+    def gather(kinds):
+        for kind in kinds:
             for ring in (0, 1):
-                ring_wait(ring, step)
-                if step < half:
-                    ring_send(ring, step + 1)
-                sib_send(ring, step)
-        sib_wait(0, step)
-        for when_, r in order:
-            if when_ == step:
-                target_chunk(r)
-        sib_wait(1, step)
+                ring_wait(ring, kind)
+                for later in next_kinds.get(kind, ()):
+                    ring_send(ring, later)
+                if kind != 6:
+                    sib_send(ring, kind if kind < 6 else 6)
+        for kind in kinds:
+            for ring in (0, 1):
+                if kind != 7:
+                    sib_wait(ring, kind)
+
+    for ring in (0, 1):
+        sib_wait(ring, None)
+    gather(first_kinds)
+    target_stage(0)
+    if Z == 8:
+        gather((4, 5))
+        target_stage(1)
+        gather((6, 7))
+        target_stage(2)
 
     load_d.wait()
-    d_part = matmul(a_d[...].reshape(s.ROWS, s.F), dhead[...], NT)
-    for a in range(s.VD // L):
-        dfull[a] = d_part[:, a * L:(a + 1) * L]
-    zpx = Z // X
-    for zz in range(Z):
-        for cc in range(2):
-            for j in range(R0):
-                to = pl.ds(((zz % zpx) * 2 + cc) * G + j, Y, stride=R0)
-                for a in range(s.VD // L):
-                    dp[zz // zpx, a, to, :] = dfull[
-                        a, pl.ds((cc * Z + zz) * R0 + j, Y, stride=2 * G), :
-                    ]
+    dp[...] = matmul(a_d[...].reshape(s.ROWS, s.F), dhead[...], NT).reshape(X, s.CH, s.VD)
     for k in range(1, X):
         send(dp.at[lax.rem(x - k + X, X)], dr.at[k], sem_ds.at[k], sem_dr.at[k], v,
              lax.rem(x - k + X, X))
 
-    for k in range(1, X):
-        arrived(tr.at[k], sem_tr.at[k])
-    lt = tp[x]
-    for k in range(1, X):
-        lt = lt + tr[k]
+    pieces = []
+    for st in range(len(stages) - 1):
+        for k in range(1, X):
+            arrived(tr[st].at[k], sem_tr.at[st, k])
+        piece = tp[st][x]
+        for k in range(1, X):
+            piece = piece + tr[st][k]
+        pieces.append(piece)
+    lt = jnp.concatenate(pieces, axis=0) if len(pieces) > 1 else pieces[0]
     live_limit = s.VT * V - s.VT // 2
     live = iota((1, s.VT), 1) + v * s.VT < live_limit
     tm = jnp.max(jnp.where(live, lt, FAR_BELOW), axis=1, keepdims=True)
@@ -303,38 +323,64 @@
 
     s_out[...] = jnp.zeros_like(s_out)
 
+    lr, lz = R0.bit_length() - 1, Z.bit_length() - 1
+    lx = zpx.bit_length() - 1
+
+    def spot(src, dst):
+        j_ = src & (R0 - 1)
+        z_ = (src >> lr) & (zpx - 1)
+        c_ = (src >> (lr + lx)) & 1
+        c_ = c_ + c - 2 * c * c_
+        i_ = src >> (lr + lx + 1)
+        turn = jnp.zeros_like(src)
+        for i, other in enumerate(turns):
+            turn = jnp.where(i_ == i, other % Y, turn)
+        y_ = (turn + y) & (Y - 1)
+        return (((z_ * 2 + c_) * Y + y_) << lr) + j_ == dst
+
+    eye = iota((s.CH, 128), 0) == iota((s.CH, 128), 1)
+    eye_t = spot(iota((s.CH, 128), 0), iota((s.CH, 128), 1))
+
+    def to_row(col, mask=eye):
+        return jnp.sum(jnp.where(mask, col, 0.0), axis=0, keepdims=True)
+
+    def to_col(row):
+        return jnp.sum(jnp.where(eye, row, 0.0), axis=1, keepdims=True)
+
     @pl.when(owner)
     def _():
         te16 = te.astype(BF)
+        square = (s.CH, s.CH)
+        order = jnp.where(spot(iota(square, 1), iota(square, 0)), 1.0, 0.0).astype(BF)
+        te16 = matmul(order, te16, NN).astype(BF)
         for i in range(2):
             s_out[i] = matmul(te16, sel[:, i * s.VD:(i + 1) * s.VD], NN).astype(BF)
 
     mass_here = jnp.sum(s_out[0].astype(F32) + s_out[1].astype(F32), axis=1, keepdims=True)
-
-    eye = iota((s.CH, 128), 0) == iota((s.CH, 128), 1)
-
-    def to_row(col):
-        return jnp.sum(jnp.where(eye, col, 0.0), axis=0, keepdims=True)
-
-    def to_col(row):
-        return jnp.sum(jnp.where(eye, row, 0.0), axis=1, keepdims=True)
-
-    st_own[...] = jnp.broadcast_to(to_row(tm), st_own.shape)
-
-    @pl.when(owner)
-    def _():
-        rcopy(s_out.at[1], s_in, sem_ss.at[1], sem_sr.at[0], 2 * v + 1, x).start()
-        rcopy(st_own, st_in, sem_ss.at[3], sem_sr.at[1], 2 * v + 1, x).start()
-
-        @pl.when(v > 0)
+    tm_row, ts_row = to_row(tm, eye_t), to_row(ts, eye_t)
+    st_own[...] = jnp.broadcast_to(tm_row, st_own.shape)
+
+    def soft_copies(action):
+        @pl.when(owner)
         def _():
-            rcopy(s_out.at[0], s_in, sem_ss.at[0], sem_sr.at[0], 2 * v, x).start()
-            rcopy(st_own, st_in, sem_ss.at[2], sem_sr.at[1], 2 * v, x).start()
+            action(rcopy(s_out.at[1], s_in, sem_ss.at[1], sem_sr.at[0], 2 * v + 1, x))
+            action(rcopy(st_own, st_in, sem_ss.at[3], sem_sr.at[1], 2 * v + 1, x))
+
+            @pl.when(v > 0)
+            def _():
+                action(rcopy(s_out.at[0], s_in, sem_ss.at[0], sem_sr.at[0], 2 * v, x))
+                action(rcopy(st_own, st_in, sem_ss.at[2], sem_sr.at[1], 2 * v, x))
+
+    def soft_send():
+        soft_copies(lambda cp: cp.start())
+        drains.append(lambda: soft_copies(lambda cp: cp.wait_send()))
 
         @pl.when(v == 0)
         def _():
             s_in[...] = s_out[0]
             st_in[...] = st_own[...]
+
+    soft_send()
 
     valid = dvalid[...] > 0
     for k in range(1, X):
@@ -342,15 +388,13 @@
     l_d = dp[x]
     for k in range(1, X):
         l_d = l_d + dr[k]
-    l_d = jnp.concatenate([l_d[a] for a in range(s.VD // L)], axis=1)
     ld[...] = l_d
     dm = jnp.max(jnp.where(valid, l_d, FAR_BELOW), axis=1, keepdims=True)
     ds = jnp.sum(jnp.where(valid, jnp.exp(l_d - dm), 0.0), axis=1, keepdims=True)
 
     zero_row = jnp.zeros((5, 128), F32)
-    tmr = to_row(tm)
-    maxes = jnp.concatenate([tmr, tmr, to_row(dm), zero_row], axis=0)
-    sums = jnp.concatenate([to_row(ts), to_row(mass_here), to_row(ds), zero_row], axis=0)
+    maxes = jnp.concatenate([tm_row, tm_row, to_row(dm), zero_row], axis=0)
+    sums = jnp.concatenate([ts_row, to_row(mass_here), to_row(ds), zero_row], axis=0)
 
     def exchange(buf, slot, n, peer, ssem, rsem):
         for k in range(1, n):
@@ -414,7 +458,6 @@
     cross_send(0, cross)
     shape = (s.ROWS, s.ROWS)
     dpos, tpos = iota(shape, 0), iota(shape, 1)
-    lr, lz = R0.bit_length() - 1, Z.bit_length() - 1
     dj = dpos & (R0 - 1)
     dz = (dpos >> lr) & (Z - 1)
     dc = (dpos >> (lr + lz)) & 1
@@ -451,7 +494,7 @@
             q[k] = (keep[to] + jr[to].astype(F32)).astype(BF)
             send(q.at[k], qr.at[k], sem_qs.at[i, k], sem_qr.at[i, k], peer(k))
 
-    ghead[...] = matmul(ga_d[...].reshape(s.ROWS, s.VD), a_d[...].reshape(s.ROWS, s.F), TN).astype(
+    ghead[...] = matmul(ga_t[...].reshape(s.ROWS, s.VD), a_d[...].reshape(s.ROWS, s.F), TN).astype(
         BF
     )
     store = pltpu.make_async_copy(ghead, ghead_out, sem_out)
@@ -477,7 +520,7 @@
 
     total_cross = to_col(cross_wait(2)[0:1])
     loss = mass * lse - total_cross
-    shape = (s.CH, 128)
+    shape = (s.CH, s.CH)
     src, dst = iota(shape, 0), iota(shape, 1)
     sj = src & (R0 - 1)
     sy = (src >> lr) & (Y - 1)
@@ -497,21 +540,7 @@
                 0, pl.ds(k, R0, stride=nk), :
             ].astype(BF)
 
-    for cp in sends:
-        cp.wait_send()
-    for k in range(1, X):
-        rcopy(tr.at[k], tr.at[k], sem_ts.at[k], sem_ts.at[k], v, x).wait_send()
-
-    @pl.when(owner)
-    def _():
-        rcopy(s_out.at[1], s_in, sem_ss.at[1], sem_sr.at[0], 2 * v + 1, x).wait_send()
-        rcopy(st_own, st_in, sem_ss.at[3], sem_sr.at[1], 2 * v + 1, x).wait_send()
-
-        @pl.when(v > 0)
-        def _():
-            rcopy(s_out.at[0], s_in, sem_ss.at[0], sem_sr.at[0], 2 * v, x).wait_send()
-            rcopy(st_own, st_in, sem_ss.at[2], sem_sr.at[1], 2 * v, x).wait_send()
-
+    finish()
     store.wait()
 
 
@@ -522,16 +551,19 @@
     )
     vm = pltpu.VMEM
     dma = pltpu.SemaphoreType.DMA
+    stage_rows = (40, 16, 8) if Z == 8 else (CH, 8, 8)
     scratch = [
+        vm((s.R0, F), BF), vm((s.R0, F), BF),
+        vm((1, VD), jnp.int32), vm((1, VD), jnp.int32),
         vm((VT, F), BF), vm((VD, F), BF),
         vm((W // L, G, L), F32), vm((W // L, G * Y, L), F32),
         vm((Y, G, W), BF), vm((Z, G, W), BF),
         vm((2 * Z, G, F), BF), vm((2 * Y, G, F), BF),
         vm((8, VD), jnp.int32), vm((2, 8, VD), jnp.int32),
         vm((VT, 2 * VD), BF),
-        vm((X, CH, VT), F32), vm((X, CH, VT), F32),
-        vm((VD // L, s.ROWS, L), F32),
-        vm((X, VD // L, CH, L), F32), vm((X, VD // L, CH, L), F32),
+        *[vm((X, n, VT), F32) for n in stage_rows * 2],
+        vm((s.ROWS, VT), F32),
+        vm((X, CH, VD), F32), vm((X, CH, VD), F32),
         vm((CH, VD), F32),
         vm((2, CH, VD), BF), vm((CH, VD), BF),
         vm((8, 128), F32), vm((8, 128), F32),
@@ -545,36 +577,74 @@
         vm((Z, G, H), BF), vm((Y, G, H), BF),
         vm((2, Y, G, W2), BF), vm((2, Y, G, W2), BF),
         vm((VD, F), BF),
-        dma((2,)),
+        dma((6,)),
         dma((2, Y)), dma((2, Y)),
-        dma((2, 2, Z // 2)), dma((2, 2, Z // 2)),
-        dma((2, Z)), dma((2, Z)),
+        dma((2, 8)), dma((2, 8)),
+        dma((2, 8)), dma((2, 8)),
         dma, dma((2,)),
-        dma((X,)), dma((X,)), dma((X,)), dma((X,)),
+        dma((3, X)), dma((3, X)), dma((X,)), dma((X,)),
         dma((4,)), dma((2,)),
         dma((3, Z)), dma((3, Z)), dma((3, Z)), dma((3, Z)),
         dma((X,)), dma((X,)),
         dma((2,)), dma((2,)), dma((2, Z)), dma((2, Z)), dma((2, Z)), dma((2, Z)),
         dma,
     ]
-    any_ = pl.BlockSpec(memory_space=pl.ANY)
+    hbm = pl.BlockSpec(memory_space=pltpu.HBM)
     vmem = pl.BlockSpec(memory_space=pltpu.VMEM)
     smem = pl.BlockSpec(memory_space=pltpu.SMEM)
     loss, gh, ghead = pl.pallas_call(
         functools.partial(body, s),
         out_shape=(
-            jax.ShapeDtypeStruct((1, 128), F32),
+            jax.ShapeDtypeStruct((1, CH), F32),
             jax.ShapeDtypeStruct((s.R0, F), BF),
             jax.ShapeDtypeStruct((VD, F), BF),
         ),
-        in_specs=[vmem, vmem, any_, any_, vmem, vmem, smem],
-        out_specs=(vmem, vmem, any_),
+        in_specs=[hbm, hbm, hbm, hbm, hbm, hbm, smem],
+        out_specs=(vmem, vmem, hbm),
         scratch_shapes=scratch,
         compiler_params=pltpu.CompilerParams(
-            collective_id=0, has_side_effects=True, vmem_limit_bytes=48 * 1024 * 1024
+            collective_id=0, has_side_effects=True, vmem_limit_bytes=63 * 1024 * 1024
         ),
     )(th, dh, thead, dhead, dmap.reshape(1, VD), dvalid.reshape(1, VD), scale.reshape(1, 1))
-    return loss[0, :CH], gh, ghead
+    return hand_out(ghead, gh, loss)
+
+
+def hand_out(*arrays):
+    def copy(*refs):
+        n = len(arrays)
+        held, sems = refs[2 * n:3 * n], refs[3 * n]
+        moves = []
+        for src, mid, dst in zip(refs[:n], held, refs[n:2 * n]):
+            rows = src.shape[0]
+            cut = rows // 4 if rows >= 128 else rows
+            for i in range(0, rows, cut):
+                part = pl.ds(i, cut)
+                k = len(moves)
+                moves.append((
+                    pltpu.make_async_copy(src.at[part], mid.at[part], sems.at[0, k]),
+                    pltpu.make_async_copy(mid.at[part], dst.at[part], sems.at[1, k]),
+                ))
+        for come, _ in moves:
+            come.start()
+        for come, go in moves:
+            come.wait()
+            go.start()
+        for _, go in moves:
+            go.wait()
+
+    hbm = pl.BlockSpec(memory_space=pltpu.HBM)
+    ghead, gh, loss = pl.pallas_call(
+        copy,
+        out_shape=tuple(jax.ShapeDtypeStruct(a.shape, a.dtype) for a in arrays),
+        in_specs=[hbm] * len(arrays),
+        out_specs=(hbm,) * len(arrays),
+        scratch_shapes=[
+            *[pltpu.VMEM(a.shape, a.dtype) for a in arrays],
+            pltpu.SemaphoreType.DMA((2, 8)),
+        ],
+        compiler_params=pltpu.CompilerParams(vmem_limit_bytes=63 * 1024 * 1024),
+    )(*arrays)
+    return loss.reshape(loss.shape[1]), gh, ghead
 
 
 def solution(mesh):

time: 91.4 us -> 78.7 us (0.86)
  local copies, waits for them, and re-layouts: 7.79 us -> 0 us
  Pallas kernels: 82 us -> 77.3 us
    unnamed x14 -> x0, local copies, waits for them, and re-layouts: 7.27 us -> none
    pallas_call x1, Pallas kernels: 82 us -> 75.2 us  [on_device(): pl.pallas_call(functools.partial(body, s), out_shape=(jax.ShapeDtypeStruc...]
    pallas_call x0 -> x1, Pallas kernels: none -> 2.06 us  [hand_out(): pl.pallas_call(copy, out_shape=tuple((jax.ShapeDtypeStruct(a.shape, a.dty...]
where the time goes in v2:
time: 78.7 us; the launch traced here: 78.6 us
  Pallas kernels  77.3 us (98%)
  between operations  1.29 us (2%)
    pallas_call x1, Pallas kernels, on_device(): pl.pallas_call(functools.partial(body, s), out_shape=(jax.ShapeDtypeStruc...  75.2 us
    pallas_call x1, Pallas kernels, hand_out(): pl.pallas_call(copy, out_shape=tuple((jax.ShapeDtypeStruct(a.shape, a.dty...  2.06 us

profile of v2, /device:TPU:1, one launch (start us, length us, event | category | flops | bytes accessed | tf_op | source)
XLA Modules:
  0.0 78.6 jit_solution(7701276328163364488)
XLA Ops:
  1.3 75.2 %shard_map.94 = (f32[1,64]{1,0:T(1,128)}, bf16[2,2048]{1,0:T(2,128)(2,1)}, bf16[256,2048]{1,0:T(8,128)(2,1)}) custom-call(bf16[2,2048]{1,0:T(2,128)(2,1)} %th_hbm.1, bf16[2,2048]{1,0:T(2,128)(2,1)} %dh_hbm.1, bf16[640,2048]{1,0:T(8,128)(2,1)} %thead_hbm.1, bf16[256,2048]{1,0:T(8,128)(2,1)} %dhead_hbm.1, s32[1,256]{1,0:T(1,128)} %bitcast.5, ...), custom_call_target="tpu_custom_call" | custom-call | tf_op jit(solution)/shard_map/pallas_call | solution.py:595
  76.5 2.1 %shard_map.95 = (bf16[256,2048]{1,0:T(8,128)(2,1)}, bf16[2,2048]{1,0:T(2,128)(2,1)}, f32[1,64]{1,0:T(1,128)}) custom-call(bf16[256,2048]{1,0:T(8,128)(2,1)} %get-tuple-element.9.refs_0_, bf16[2,2048]{1,0:T(2,128)(2,1)} %get-tuple-element.10.refs_1_, f32[1,64]{1,0:T(1,128)} %get-tuple-element.11.refs_2_), custom_call_target="tpu_custom_call" | custom-call | tf_op jit(solution)/shard_map/pallas_call | solution.py:636

commit v3 on v2

--- a/solution.py
+++ b/solution.py
@@ -24,6 +24,10 @@
 
 def iota(shape, dim):
     return lax.broadcasted_iota(jnp.int32, shape, dim)
+
+
+def far_first(n):
+    return sorted(range(1, n), key=lambda k: -min(k, n - k))
 
 
 class Sizes:
@@ -46,8 +50,8 @@
     s,
     th_hbm, dh_hbm, thead_hbm, dhead_hbm, dmap_hbm, dvalid_hbm, scale,
     loss_out, gh_out, ghead_out,
-    th, dh, dmap, dvalid, thead, dhead, stage, stage_big, t0, d0, a_t, a_d, map_own, map_in, sel,
-    tp0, tp1, tp2, tr0, tr1, tr2, tfull, dp, dr, ld, s_out, s_in, st_own, st_in, f0, f1, f2, c0, c1, c2,
+    th, dh, dmap, dvalid, thead, dhead, stage, stage_big, t0, d0, a_t, a_d, map_own, map_in, sel, used,
+    tp0, tp1, tp2, tr0, tr1, tr2, tfull, dp, dr, ld, s_out, s_in, st_own, st_in, f1, f2, c1, c2,
     ga_t, ga_d, keep_t, keep_d, js_t, js_d, jr_t, jr_d, q_t, q_d, qr_t, qr_d,
     w_out, w_in, ghead,
     sem_head, sem_l1s, sem_l1r, sem_rs, sem_rr, sem_sibs, sem_sibr, sem_ms, sem_mr,
@@ -99,6 +103,35 @@
         for drain in drains:
             drain()
 
+    owner = v < V // 2
+    owner_of = lax.div(v, 2)
+
+    barrier = pltpu.get_barrier_semaphore()
+
+    def hello(vv, xx):
+        pl.semaphore_signal(barrier, inc=1, device_id=(vv, xx), device_id_type=MESH)
+
+    @pl.when(v > 0)
+    def _():
+        hello(owner_of, x)
+
+    @pl.when(owner)
+    def _():
+        hello(2 * v + 1, x)
+
+    @pl.when(jnp.logical_and(owner, v > 0))
+    def _():
+        hello(2 * v, x)
+
+    for k in far_first(Y):
+        for core in (0, 1):
+            hello(at(z, lax.rem(y + k, Y), core), x)
+    for k in far_first(Z):
+        hello(z_peer(k), x)
+    hello(sib, x)
+    for k in range(1, X):
+        hello(v, x_peer(k))
+
     small = [
         pltpu.make_async_copy(src, dst, sem_head.at[2 + i])
         for i, (src, dst) in enumerate(
@@ -112,34 +145,6 @@
     load_t.start()
     load_d.start()
 
-    owner = v < V // 2
-    owner_of = lax.div(v, 2)
-
-    barrier = pltpu.get_barrier_semaphore()
-
-    def hello(vv, xx):
-        pl.semaphore_signal(barrier, inc=1, device_id=(vv, xx), device_id_type=MESH)
-
-    for k in range(1, Y):
-        hello(y_peer(k), x)
-    for k in range(1, Z):
-        hello(z_peer(k), x)
-    hello(sib, x)
-    for k in range(1, X):
-        hello(v, x_peer(k))
-
-    @pl.when(v > 0)
-    def _():
-        hello(owner_of, x)
-
-    @pl.when(owner)
-    def _():
-        hello(2 * v + 1, x)
-
-    @pl.when(jnp.logical_and(owner, v > 0))
-    def _():
-        hello(2 * v, x)
-
     for cp in small:
         cp.wait()
 
@@ -156,10 +161,10 @@
     live_owner = owner.astype(jnp.int32)
     live_v = (v > 0).astype(jnp.int32)
     pl.semaphore_wait(
-        barrier, (Y - 1) + (Z - 1) + 1 + (X - 1) + live_v + live_owner * (1 + live_v)
-    )
-
-    for k in range(1, Z):
+        barrier, 2 * (Y - 1) + (Z - 1) + 1 + (X - 1) + live_v + live_owner * (1 + live_v)
+    )
+
+    for k in far_first(Z):
         send(t0.at[z], t0.at[z], sem_l1s.at[0, k], sem_l1r.at[0, k], z_peer(k))
         send(d0.at[y], d0.at[y], sem_l1s.at[1, k], sem_l1r.at[1, k], y_peer(k))
 
@@ -245,6 +250,8 @@
     relayout(d0, a_d, z * 2 + c)
     ring_start(1)
 
+    used[...] = jnp.zeros_like(used)
+
     @pl.when(owner)
     def _():
         arrived(map_in.at[1], sem_mr.at[1])
@@ -257,6 +264,7 @@
         for i in range(2):
             hit = ids == jnp.broadcast_to(map_in[i, 0:1, :], (s.VT, s.VD))
             sel[:, i * s.VD:(i + 1) * s.VD] = jnp.where(hit, 1.0, 0.0).astype(BF)
+        used[...] = matmul(jnp.ones((8, 2 * s.VD), BF), sel[...], NT)
 
     load_t.wait()
 
@@ -290,38 +298,46 @@
                 if kind != 7:
                     sib_wait(ring, kind)
 
+    def draft_rows():
+        whole = matmul(a_d[...].reshape(s.ROWS, s.F), dhead[...], NT)
+        for zz in range(Z):
+            dp[zz] = whole[zz * 2 * G:(zz + 1) * 2 * G]
+        for k in range(1, X):
+            to = lax.rem(x - k + X, X)
+            for i in range(zpx):
+                send(dp.at[to * zpx + i], dr.at[k, i], sem_ds.at[k, i], sem_dr.at[k, i], v, to)
+
     for ring in (0, 1):
         sib_wait(ring, None)
     gather(first_kinds)
     target_stage(0)
+    load_d.wait()
     if Z == 8:
         gather((4, 5))
         target_stage(1)
         gather((6, 7))
         target_stage(2)
-
-    load_d.wait()
-    dp[...] = matmul(a_d[...].reshape(s.ROWS, s.F), dhead[...], NT).reshape(X, s.CH, s.VD)
-    for k in range(1, X):
-        send(dp.at[lax.rem(x - k + X, X)], dr.at[k], sem_ds.at[k], sem_dr.at[k], v,
-             lax.rem(x - k + X, X))
-
-    pieces = []
+    draft_rows()
+
+    live_limit = s.VT * V - s.VT // 2
+    live = iota((1, s.VT), 1) + v * s.VT < live_limit
+    by_stage = []
     for st in range(len(stages) - 1):
         for k in range(1, X):
             arrived(tr[st].at[k], sem_tr.at[st, k])
-        piece = tp[st][x]
+        lt = tp[st][x]
         for k in range(1, X):
-            piece = piece + tr[st][k]
-        pieces.append(piece)
-    lt = jnp.concatenate(pieces, axis=0) if len(pieces) > 1 else pieces[0]
-    live_limit = s.VT * V - s.VT // 2
-    live = iota((1, s.VT), 1) + v * s.VT < live_limit
-    tm = jnp.max(jnp.where(live, lt, FAR_BELOW), axis=1, keepdims=True)
-    te = jnp.where(live, jnp.exp(lt - tm), 0.0)
-    ts = jnp.sum(te, axis=1, keepdims=True)
-
-    s_out[...] = jnp.zeros_like(s_out)
+            lt = lt + tr[st][k]
+        high = jnp.max(jnp.where(live, lt, FAR_BELOW), axis=1, keepdims=True)
+        grown = jnp.where(live, jnp.exp(lt - high), 0.0)
+        rounded = grown.astype(BF).astype(F32)
+        by_stage.append((
+            high, jnp.sum(grown, axis=1, keepdims=True), rounded,
+            jnp.sum(rounded * used[0:1], axis=1, keepdims=True),
+        ))
+    tm, ts, te, mass_here = (
+        jnp.concatenate(cols, axis=0) if len(cols) > 1 else cols[0] for cols in zip(*by_stage)
+    )
 
     lr, lz = R0.bit_length() - 1, Z.bit_length() - 1
     lx = zpx.bit_length() - 1
@@ -344,21 +360,22 @@
     def to_row(col, mask=eye):
         return jnp.sum(jnp.where(mask, col, 0.0), axis=0, keepdims=True)
 
-    def to_col(row):
-        return jnp.sum(jnp.where(eye, row, 0.0), axis=1, keepdims=True)
+    eye_hi = iota((s.CH, 128), 0) + 64 == iota((s.CH, 128), 1)
+
+    def to_col(row, mask=eye):
+        return jnp.sum(jnp.where(mask, row, 0.0), axis=1, keepdims=True)
+
+    te16 = te.astype(BF)
+    tm_row, ts_row = to_row(tm, eye_t), to_row(ts, eye_t)
+    st_own[...] = tm_row
 
     @pl.when(owner)
     def _():
-        te16 = te.astype(BF)
         square = (s.CH, s.CH)
         order = jnp.where(spot(iota(square, 1), iota(square, 0)), 1.0, 0.0).astype(BF)
-        te16 = matmul(order, te16, NN).astype(BF)
+        rows = matmul(order, te16, NN).astype(BF)
         for i in range(2):
-            s_out[i] = matmul(te16, sel[:, i * s.VD:(i + 1) * s.VD], NN).astype(BF)
-
-    mass_here = jnp.sum(s_out[0].astype(F32) + s_out[1].astype(F32), axis=1, keepdims=True)
-    tm_row, ts_row = to_row(tm, eye_t), to_row(ts, eye_t)
-    st_own[...] = jnp.broadcast_to(tm_row, st_own.shape)
+            s_out[i] = matmul(rows, sel[:, i * s.VD:(i + 1) * s.VD], NN).astype(BF)
 
     def soft_copies(action):
         @pl.when(owner)
@@ -383,53 +400,78 @@
     soft_send()
 
     valid = dvalid[...] > 0
-    for k in range(1, X):
-        arrived(dr.at[k], sem_dr.at[k])
-    l_d = dp[x]
-    for k in range(1, X):
-        l_d = l_d + dr[k]
+    blocks = []
+    for i in range(zpx):
+        block = dp[x * zpx + i]
+        for k in range(1, X):
+            arrived(dr.at[k, i], sem_dr.at[k, i])
+            block = block + dr[k, i]
+        blocks.append(block)
+    l_d = jnp.concatenate(blocks, axis=0) if zpx > 1 else blocks[0]
     ld[...] = l_d
     dm = jnp.max(jnp.where(valid, l_d, FAR_BELOW), axis=1, keepdims=True)
     ds = jnp.sum(jnp.where(valid, jnp.exp(l_d - dm), 0.0), axis=1, keepdims=True)
 
-    zero_row = jnp.zeros((5, 128), F32)
-    maxes = jnp.concatenate([tm_row, tm_row, to_row(dm), zero_row], axis=0)
-    sums = jnp.concatenate([ts_row, to_row(mass_here), to_row(ds), zero_row], axis=0)
-
-    def exchange(buf, slot, n, peer, ssem, rsem):
-        for k in range(1, n):
-            send(buf.at[slot], buf.at[slot], ssem.at[k], rsem.at[k], peer(k))
-
-    def exchange_wait(buf, slot, n, rsem):
-        for k in range(1, n):
-            arrived(buf.at[lax.rem(slot + n - k, n)], rsem.at[k])
-
-    hops = (
-        (f0, c0, c, 2, lambda k: sib),
-        (f1, c1, y, Y, y_peer),
-        (f2, c2, z, Z, z_peer),
-    )
-    for h, (buf, _, slot, n, peer) in enumerate(hops):
-        buf[slot, 0] = maxes
-        buf[slot, 1] = sums
-        exchange(buf, slot, n, peer, sem_fs.at[h], sem_fr.at[h])
-        exchange_wait(buf, slot, n, sem_fr.at[h])
-        maxes = buf[0, 0]
+    maxes = tm_row + to_row(dm, eye_hi)
+    sums = ts_row + to_row(ds, eye_hi)
+    masses = to_row(mass_here, eye_t)
+
+    def all_of_y():
+        own_slot = y * 2 + c
+        out = [
+            (at(z, lax.rem(y + k, Y), core), 2 * k + core, 2 * k + c)
+            for k in far_first(Y) for core in (0, 1)
+        ] + [(sib, 0, c)]
+        came = [(sib - at(z, 0, 0), 1 - c)] + [
+            (lax.rem(y + Y - k, Y) * 2 + core, 2 * k + core)
+            for k in far_first(Y)[::-1] for core in (0, 1)
+        ]
+        return own_slot, 2 * Y, out, came
+
+    def all_of_z():
+        out = [(z_peer(k), k, k) for k in far_first(Z)]
+        came = [(lax.rem(z + Z - k, Z), k) for k in far_first(Z)[::-1]]
+        return z, Z, out, came
+
+    hops = (all_of_y(), all_of_z())
+
+    def exchange(h, bufs, ssem, rsem, value):
+        own_slot, _, out, _ = hops[h]
+        bufs[h][own_slot] = value
+        for to, i, k in out:
+            ref = bufs[h].at[own_slot]
+            send(ref, ref, ssem.at[h, i], rsem.at[h, k], to)
+
+    def exchange_wait(h, bufs, rsem):
+        for slot, k in hops[h][3]:
+            arrived(bufs[h].at[slot], rsem.at[h, k])
+
+    stats = (f1, f2)
+    exchange(0, stats, sem_fs, sem_fr, jnp.concatenate([maxes, sums, masses], axis=1))
+
+    for h in range(2):
+        buf, n = stats[h], hops[h][1]
+        exchange_wait(h, stats, sem_fr)
+        maxes = buf[0, :, 0:L]
         for i in range(1, n):
-            maxes = jnp.maximum(maxes, buf[i, 0])
-        sums = buf[0, 1] * jnp.exp(buf[0, 0] - maxes)
-        for i in range(1, n):
-            sums = sums + buf[i, 1] * jnp.exp(buf[i, 0] - maxes)
+            maxes = jnp.maximum(maxes, buf[i, :, 0:L])
+        sums, masses = jnp.zeros_like(maxes), jnp.zeros_like(maxes)
+        for i in range(n):
+            share = jnp.exp(buf[i, :, 0:L] - maxes)
+            sums = sums + buf[i, :, L:2 * L] * share
+            masses = masses + buf[i, :, 2 * L:3 * L] * share
+        if h == 0:
+            exchange(1, stats, sem_fs, sem_fr, jnp.concatenate([maxes, sums, masses], axis=1))
 
     @pl.when(v > 0)
     def _():
         arrived(s_in, sem_sr.at[0])
         arrived(st_in, sem_sr.at[1])
 
-    t_max, t_total = maxes[0:1], sums[0:1]
-    factor = to_col(jnp.exp(st_in[0:1] - t_max) / t_total)
-    mass = to_col(sums[1:2] / t_total)
-    lse = to_col(maxes[2:3] + jnp.log(sums[2:3]))
+    t_total = to_col(sums)
+    factor = jnp.exp(to_col(st_in[...]) - to_col(maxes)) / t_total
+    mass = to_col(masses) / t_total
+    lse = to_col(maxes, eye_hi) + jnp.log(to_col(sums, eye_hi))
     soft = s_in[...].astype(F32) * factor
     l_d = ld[...]
     grad = scale[0, 0] * (jnp.exp(l_d - lse) * mass - soft)
@@ -440,19 +482,18 @@
         chunk = ga_t.at[pl.ds(x * s.SPC, s.SPC)]
         send(chunk, chunk, sem_gs.at[k], sem_gr.at[k], v, x_peer(k))
 
-    cross = jnp.broadcast_to(to_row(jnp.sum(soft * l_d, axis=1, keepdims=True)), (8, 128))
+    cross = to_row(jnp.sum(soft * l_d, axis=1, keepdims=True))
+
+    cross_bufs = (c1, c2)
 
     def cross_send(h, value):
-        _, buf, slot, n, peer = hops[h]
-        buf[slot] = value
-        exchange(buf, slot, n, peer, sem_cs.at[h], sem_cr.at[h])
+        exchange(h, cross_bufs, sem_cs, sem_cr, value)
 
     def cross_wait(h):
-        _, buf, slot, n, _ = hops[h]
-        exchange_wait(buf, slot, n, sem_cr.at[h])
-        total = buf[0]
-        for i in range(1, n):
-            total = total + buf[i]
+        exchange_wait(h, cross_bufs, sem_cr)
+        total = cross_bufs[h][0]
+        for i in range(1, hops[h][1]):
+            total = total + cross_bufs[h][i]
         return total
 
     cross_send(0, cross)
@@ -464,20 +505,17 @@
     dy = dpos >> (lr + lz + 1)
     perm = jnp.where((((dz * 2 + dc) * Y + dy) << lr) + dj == tpos, 1.0, 0.0).astype(BF)
 
-    cross_send(1, cross_wait(0))
-
     for k in range(1, X):
         other = ga_t.at[pl.ds(lax.rem(x + X - k, X) * s.SPC, s.SPC)]
         arrived(other, sem_gr.at[k])
+    def rows_of(buf, core):
+        return jnp.concatenate([buf[i * 2 + core] for i in range(Z)], axis=0)
+
+    js_t[...] = matmul(rows_of(ga_t, 1 - c), dhead[:, :H], NN).astype(BF).reshape(Z, G, H)
+    send(js_t, jr_t, sem_js.at[0], sem_jr.at[0], sib)
     ga_d[...] = (
         matmul(perm, ga_t[...].reshape(s.ROWS, s.VD), NN).astype(BF).reshape(2 * Y, G, s.VD)
     )
-
-    def rows_of(buf, core):
-        return jnp.concatenate([buf[i * 2 + core] for i in range(Z)], axis=0)
-
-    js_t[...] = matmul(rows_of(ga_t, 1 - c), dhead[:, :H], NN).astype(BF).reshape(Z, G, H)
-    send(js_t, jr_t, sem_js.at[0], sem_jr.at[0], sib)
     js_d[...] = matmul(rows_of(ga_d, 1 - c), dhead[:, H:], NN).astype(BF).reshape(Y, G, H)
     send(js_d, jr_d, sem_js.at[1], sem_jr.at[1], sib)
     keep_t[...] = matmul(rows_of(ga_t, c), dhead[:, :H], NN).reshape(Z, G, H)
@@ -487,9 +525,10 @@
         (0, jr_t, keep_t, q_t, qr_t, z, Z, z_peer, y, Y, y_peer),
         (1, jr_d, keep_d, q_d, qr_d, y, Y, y_peer, z, Z, z_peer),
     )
-    for i, jr, keep, q, qr, pos, n, peer, _, _, _ in parts:
+    for i, jr, *_ in parts:
         arrived(jr, sem_jr.at[i])
-        for k in range(1, n):
+    for k in far_first(Z):
+        for i, jr, keep, q, qr, pos, n, peer, _, _, _ in parts:
             to = lax.rem(pos + k, n)
             q[k] = (keep[to] + jr[to].astype(F32)).astype(BF)
             send(q.at[k], qr.at[k], sem_qs.at[i, k], sem_qr.at[i, k], peer(k))
@@ -500,25 +539,25 @@
     store = pltpu.make_async_copy(ghead, ghead_out, sem_out)
     store.start()
 
-    cross_send(2, cross_wait(1))
+    cross_send(1, cross_wait(0))
 
     for i, jr, keep, q, qr, pos, n, peer, pos2, n2, peer2 in parts:
         total = keep[pos] + jr[pos].astype(F32)
-        for k in range(1, n):
+        for k in far_first(n)[::-1]:
             arrived(qr.at[k], sem_qr.at[i, k])
             total = total + qr[k].astype(F32)
         for k in range(nk):
             stage_big[0, pl.ds(k, G, stride=nk), :] = total[:, k * W2:(k + 1) * W2]
         for p in range(n2):
             w_out[i, p] = stage_big[0, p * G:(p + 1) * G, :].astype(BF)
-        for k in range(1, n2):
+        for k in far_first(n2):
             send(
                 w_out.at[i, lax.rem(pos2 + k, n2)], w_in.at[i, k],
                 sem_ws.at[i, k], sem_wr.at[i, k], peer2(k),
             )
         w_in[i, 0] = w_out[i, pos2]
 
-    total_cross = to_col(cross_wait(2)[0:1])
+    total_cross = to_col(cross_wait(1))
     loss = mass * lse - total_cross
     shape = (s.CH, s.CH)
     src, dst = iota(shape, 0), iota(shape, 1)
@@ -560,15 +599,15 @@
         vm((Y, G, W), BF), vm((Z, G, W), BF),
         vm((2 * Z, G, F), BF), vm((2 * Y, G, F), BF),
         vm((8, VD), jnp.int32), vm((2, 8, VD), jnp.int32),
-        vm((VT, 2 * VD), BF),
+        vm((VT, 2 * VD), BF), vm((8, VT), F32),
         *[vm((X, n, VT), F32) for n in stage_rows * 2],
         vm((s.ROWS, VT), F32),
-        vm((X, CH, VD), F32), vm((X, CH, VD), F32),
+        vm((Z, 2 * G, VD), F32), vm((X, Z // X, 2 * G, VD), F32),
         vm((CH, VD), F32),
         vm((2, CH, VD), BF), vm((CH, VD), BF),
-        vm((8, 128), F32), vm((8, 128), F32),
-        vm((2, 2, 8, 128), F32), vm((Y, 2, 8, 128), F32), vm((Z, 2, 8, 128), F32),
-        vm((2, 8, 128), F32), vm((Y, 8, 128), F32), vm((Z, 8, 128), F32),
+        vm((1, 128), F32), vm((1, 128), F32),
+        vm((2 * Y, 1, 3 * L), F32), vm((Z, 1, 3 * L), F32),
+        vm((2 * Y, 1, L), F32), vm((Z, 1, L), F32),
         vm((2 * Z, G, VD), BF), vm((2 * Y, G, VD), BF),
         vm((Z, G, H), F32), vm((Y, G, H), F32),
         vm((Z, G, H), BF), vm((Y, G, H), BF),
@@ -582,9 +621,9 @@
         dma((2, 8)), dma((2, 8)),
         dma((2, 8)), dma((2, 8)),
         dma, dma((2,)),
-        dma((3, X)), dma((3, X)), dma((X,)), dma((X,)),
+        dma((3, X)), dma((3, X)), dma((X, Z // X)), dma((X, Z // X)),
         dma((4,)), dma((2,)),
-        dma((3, Z)), dma((3, Z)), dma((3, Z)), dma((3, Z)),
+        *[dma((2, 2 * Y))] * 4,
         dma((X,)), dma((X,)),
         dma((2,)), dma((2,)), dma((2, Z)), dma((2, Z)), dma((2, Z)), dma((2, Z)),
         dma,

time: 78.7 us -> 76 us (0.966)
  Pallas kernels: 77.3 us -> 74.5 us
    pallas_call x1, Pallas kernels: 75.2 us -> 72.5 us  [on_device(): pl.pallas_call(functools.partial(body, s), out_shape=(jax.ShapeDtypeStruc...]
where the time goes in v3:
time: 76 us; the launch traced here: 75.8 us
  Pallas kernels  74.5 us (98%)
  between operations  1.29 us (2%)
    pallas_call x1, Pallas kernels, on_device(): pl.pallas_call(functools.partial(body, s), out_shape=(jax.ShapeDtypeStruc...  72.5 us
    pallas_call x1, Pallas kernels, hand_out(): pl.pallas_call(copy, out_shape=tuple((jax.ShapeDtypeStruct(a.shape, a.dty...  2.06 us

profile of v3, /device:TPU:1, one launch (start us, length us, event | category | flops | bytes accessed | tf_op | source)
XLA Modules:
  0.0 75.8 jit_solution(7745095007053896638)
XLA Ops:
  1.3 72.5 %shard_map.94 = (f32[1,64]{1,0:T(1,128)}, bf16[2,2048]{1,0:T(2,128)(2,1)}, bf16[256,2048]{1,0:T(8,128)(2,1)}) custom-call(bf16[2,2048]{1,0:T(2,128)(2,1)} %th_hbm.1, bf16[2,2048]{1,0:T(2,128)(2,1)} %dh_hbm.1, bf16[640,2048]{1,0:T(8,128)(2,1)} %thead_hbm.1, bf16[256,2048]{1,0:T(8,128)(2,1)} %dhead_hbm.1, s32[1,256]{1,0:T(1,128)} %bitcast.5, ...), custom_call_target="tpu_custom_call" | custom-call | tf_op jit(solution)/shard_map/pallas_call | solution.py:634
  73.8 2.1 %shard_map.95 = (bf16[256,2048]{1,0:T(8,128)(2,1)}, bf16[2,2048]{1,0:T(2,128)(2,1)}, f32[1,64]{1,0:T(1,128)}) custom-call(bf16[256,2048]{1,0:T(8,128)(2,1)} %get-tuple-element.9.refs_0_, bf16[2,2048]{1,0:T(2,128)(2,1)} %get-tuple-element.10.refs_1_, f32[1,64]{1,0:T(1,128)} %get-tuple-element.11.refs_2_), custom_call_target="tpu_custom_call" | custom-call | tf_op jit(solution)/shard_map/pallas_call | solution.py:675

commit v4 on v3

--- a/solution.py
+++ b/solution.py
@@ -281,7 +281,7 @@
                 tp[st][r, (b - lo) * per:(b - lo + 1) * per, :] = tfull[
                     b * G + r * per:b * G + (r + 1) * per, :
                 ]
-        for k in range(1, X):
+        for k in far_first(X):
             to = lax.rem(x - k + X, X)
             send(tp[st].at[to], tr[st].at[k], sem_ts.at[st, k], sem_tr.at[st, k], v, to)
 
@@ -302,7 +302,7 @@
         whole = matmul(a_d[...].reshape(s.ROWS, s.F), dhead[...], NT)
         for zz in range(Z):
             dp[zz] = whole[zz * 2 * G:(zz + 1) * 2 * G]
-        for k in range(1, X):
+        for k in far_first(X):
             to = lax.rem(x - k + X, X)
             for i in range(zpx):
                 send(dp.at[to * zpx + i], dr.at[k, i], sem_ds.at[k, i], sem_dr.at[k, i], v, to)
@@ -478,7 +478,7 @@
     ga_t[pl.ds(x * s.SPC, s.SPC)] = (
         jnp.where(valid, grad, 0.0).astype(BF).reshape(s.SPC, G, s.VD)
     )
-    for k in range(1, X):
+    for k in far_first(X):
         chunk = ga_t.at[pl.ds(x * s.SPC, s.SPC)]
         send(chunk, chunk, sem_gs.at[k], sem_gr.at[k], v, x_peer(k))
 
@@ -513,22 +513,21 @@
 
     js_t[...] = matmul(rows_of(ga_t, 1 - c), dhead[:, :H], NN).astype(BF).reshape(Z, G, H)
     send(js_t, jr_t, sem_js.at[0], sem_jr.at[0], sib)
+    keep_t[...] = matmul(rows_of(ga_t, c), dhead[:, :H], NN).reshape(Z, G, H)
     ga_d[...] = (
         matmul(perm, ga_t[...].reshape(s.ROWS, s.VD), NN).astype(BF).reshape(2 * Y, G, s.VD)
     )
     js_d[...] = matmul(rows_of(ga_d, 1 - c), dhead[:, H:], NN).astype(BF).reshape(Y, G, H)
     send(js_d, jr_d, sem_js.at[1], sem_jr.at[1], sib)
-    keep_t[...] = matmul(rows_of(ga_t, c), dhead[:, :H], NN).reshape(Z, G, H)
     keep_d[...] = matmul(rows_of(ga_d, c), dhead[:, H:], NN).reshape(Y, G, H)
 
     parts = (
         (0, jr_t, keep_t, q_t, qr_t, z, Z, z_peer, y, Y, y_peer),
         (1, jr_d, keep_d, q_d, qr_d, y, Y, y_peer, z, Z, z_peer),
     )
-    for i, jr, *_ in parts:
+    for i, jr, keep, q, qr, pos, n, peer, _, _, _ in parts:
         arrived(jr, sem_jr.at[i])
-    for k in far_first(Z):
-        for i, jr, keep, q, qr, pos, n, peer, _, _, _ in parts:
+        for k in far_first(n):
             to = lax.rem(pos + k, n)
             q[k] = (keep[to] + jr[to].astype(F32)).astype(BF)
             send(q.at[k], qr.at[k], sem_qs.at[i, k], sem_qr.at[i, k], peer(k))

time: 76 us -> 75.8 us (level)
  no operation moved by 1% of the time
where the time goes in v4:
time: 75.8 us; the launch traced here: 75.6 us
  Pallas kernels  74.3 us (98%)
  between operations  1.29 us (2%)
    pallas_call x1, Pallas kernels, on_device(): pl.pallas_call(functools.partial(body, s), out_shape=(jax.ShapeDtypeStruc...  72.3 us
    pallas_call x1, Pallas kernels, hand_out(): pl.pallas_call(copy, out_shape=tuple((jax.ShapeDtypeStruct(a.shape, a.dty...  2.06 us

profile of v4, /device:TPU:1, one launch (start us, length us, event | category | flops | bytes accessed | tf_op | source)
XLA Modules:
  0.0 75.6 jit_solution(57202708910813497)
XLA Ops:
  1.3 72.3 %shard_map.94 = (f32[1,64]{1,0:T(1,128)}, bf16[2,2048]{1,0:T(2,128)(2,1)}, bf16[256,2048]{1,0:T(8,128)(2,1)}) custom-call(bf16[2,2048]{1,0:T(2,128)(2,1)} %th_hbm.1, bf16[2,2048]{1,0:T(2,128)(2,1)} %dh_hbm.1, bf16[640,2048]{1,0:T(8,128)(2,1)} %thead_hbm.1, bf16[256,2048]{1,0:T(8,128)(2,1)} %dhead_hbm.1, s32[1,256]{1,0:T(1,128)} %bitcast.5, ...), custom_call_target="tpu_custom_call" | custom-call | tf_op jit(solution)/shard_map/pallas_call | solution.py:633
  73.5 2.1 %shard_map.95 = (bf16[256,2048]{1,0:T(8,128)(2,1)}, bf16[2,2048]{1,0:T(2,128)(2,1)}, f32[1,64]{1,0:T(1,128)}) custom-call(bf16[256,2048]{1,0:T(8,128)(2,1)} %get-tuple-element.9.refs_0_, bf16[2,2048]{1,0:T(2,128)(2,1)} %get-tuple-element.10.refs_1_, f32[1,64]{1,0:T(1,128)} %get-tuple-element.11.refs_2_), custom_call_target="tpu_custom_call" | custom-call | tf_op jit(solution)/shard_map/pallas_call | solution.py:674

commit v5 on v3

--- a/solution.py
+++ b/solution.py
@@ -183,18 +183,23 @@
     def _():
         map_in[0] = map_own[...]
 
-    def relayout(src, dst, slot):
-        for i in range(Y):
-            for a in range(W // L):
-                stage_big[a, i * G:(i + 1) * G, :] = src[i, :, a * L:(a + 1) * L].astype(F32)
+    def lay(src, i):
+        for a in range(W // L):
+            rows = pl.ds(pl.multiple_of(i * G, G), G)
+            stage_big[a, rows, :] = src[i, :, a * L:(a + 1) * L].astype(F32)
+
+    def relayout(src, dst, slot, pos, sem):
+        lay(src, pos)
+        for k in far_first(Y)[::-1]:
+            i = lax.rem(pos + Y - k, Y)
+            arrived(src.at[i], sem.at[k])
+            lay(src, i)
         for k in range(nk):
             for a in range(W // L):
                 cols = slice(k * W + a * L, k * W + (a + 1) * L)
                 dst[slot, :, cols] = stage_big[a, pl.ds(k, G, stride=nk), :].astype(BF)
 
-    for k in range(1, Z):
-        arrived(t0.at[lax.rem(z + Z - k, Z)], sem_l1r.at[0, k])
-    relayout(t0, a_t, 0)
+    relayout(t0, a_t, 0, z, sem_l1r.at[0])
 
     hop = (2, -2, 1, -1, 1, -1, 2, -2)
     held = (0, 0, 0, 0, -2, 2, -2, 2)
@@ -245,9 +250,7 @@
         sib_send(ring, None)
 
     ring_start(0)
-    for k in range(1, Y):
-        arrived(d0.at[lax.rem(y + Y - k, Y)], sem_l1r.at[1, k])
-    relayout(d0, a_d, z * 2 + c)
+    relayout(d0, a_d, z * 2 + c, y, sem_l1r.at[1])
     ring_start(1)
 
     used[...] = jnp.zeros_like(used)

time: 76 us -> 76 us (level)
  no operation moved by 1% of the time
where the time goes in v5:
time: 76 us; the launch traced here: 75.8 us
  Pallas kernels  74.5 us (98%)
  between operations  1.29 us (2%)
    pallas_call x1, Pallas kernels, on_device(): pl.pallas_call(functools.partial(body, s), out_shape=(jax.ShapeDtypeStruc...  72.5 us
    pallas_call x1, Pallas kernels, hand_out(): pl.pallas_call(copy, out_shape=tuple((jax.ShapeDtypeStruct(a.shape, a.dty...  2.06 us

profile of v5, /device:TPU:1, one launch (start us, length us, event | category | flops | bytes accessed | tf_op | source)
XLA Modules:
  0.0 75.8 jit_solution(1887366553976886507)
XLA Ops:
  1.3 72.5 %shard_map.94 = (f32[1,64]{1,0:T(1,128)}, bf16[2,2048]{1,0:T(2,128)(2,1)}, bf16[256,2048]{1,0:T(8,128)(2,1)}) custom-call(bf16[2,2048]{1,0:T(2,128)(2,1)} %th_hbm.1, bf16[2,2048]{1,0:T(2,128)(2,1)} %dh_hbm.1, bf16[640,2048]{1,0:T(8,128)(2,1)} %thead_hbm.1, bf16[256,2048]{1,0:T(8,128)(2,1)} %dhead_hbm.1, s32[1,256]{1,0:T(1,128)} %bitcast.5, ...), custom_call_target="tpu_custom_call" | custom-call | tf_op jit(solution)/shard_map/pallas_call | solution.py:637
  73.8 2.1 %shard_map.95 = (bf16[256,2048]{1,0:T(8,128)(2,1)}, bf16[2,2048]{1,0:T(2,128)(2,1)}, f32[1,64]{1,0:T(1,128)}) custom-call(bf16[256,2048]{1,0:T(8,128)(2,1)} %get-tuple-element.9.refs_0_, bf16[2,2048]{1,0:T(2,128)(2,1)} %get-tuple-element.10.refs_1_, f32[1,64]{1,0:T(1,128)} %get-tuple-element.11.refs_2_), custom_call_target="tpu_custom_call" | custom-call | tf_op jit(solution)/shard_map/pallas_call | solution.py:678
